TPU v7x, 32 devices: a whole 2x2x4 slice. The times are simulated.
32 devices in a mesh: runs: 16 (over z, y, x), tm: 2 (over core).
Axes of the slice: x: 2, y: 2, z: 4, core: 2. Of those that a mesh axis runs over, the one named last changes fastest.
Arguments:
- tensor: bfloat16 [256, 32, 1024], P('runs', 'tm'), may hold values from 0 to 1
- run_counts: int32 [16], P('runs'), may hold values from 4 to 16, as said below
- run_init: float32 [256, 128], P('runs'), may hold values from 0.05 to 0.5
- bin_init: float32 [1024, 128], replicated, may hold values from 0.05 to 0.5
- time_init: float32 [32, 128], P('tm'), may hold values from 0.05 to 0.5
Outputs:
- run_factor: float32 [256, 128], P('runs')
- bin_factor: float32 [1024, 128], replicated
- time_factor: float32 [32, 128], P('tm')
Inputs may be any that keep to these rules, and one draw needn't show every extreme that they name: `run_counts`: at most 16 live slots on an index of runs; some index has exactly 16.
All inputs are finite; a program needn't handle non-finite values.
Results may differ from a plain program's by a relative error of at most 0.0003.
Values sent between devices are 32-bit elements; how exact they have to be, the bound alone decides.
A program may use at most 64 MiB of HBM per device.

v0:
```python
import jax
import jax.numpy as jnp
from jax import lax
from jax.sharding import PartitionSpec as P

HIGH = lax.Precision.HIGHEST
STEP_ROWS = 8


def gram(factor):
    return jnp.dot(factor.T, factor, precision=HIGH)


def run_gram_sum(runs):
    return lax.psum(gram(runs), "runs")


def time_gram_sum(times):
    return lax.psum(gram(times), "tm")


def shards(tensor, run_counts, run_init, bin_init, time_init):
    rowcap = tensor.shape[0]
    count = run_counts[0]
    live = (jnp.arange(rowcap, dtype=jnp.int32) < count).astype(jnp.float32)[:, None]
    blocks = (count + STEP_ROWS - 1) // STEP_ROWS
    runs = run_init * live
    bins = bin_init
    times = time_init

    def sweep(step, init):
        return lax.fori_loop(0, blocks, lambda index, carry: step(index * STEP_ROWS, carry), init)

    run_gram = run_gram_sum(runs)
    bin_gram = gram(bins)
    time_gram = time_gram_sum(times)
    bins_low = bins.astype(jnp.bfloat16)

    def step(start, total):
        block = lax.dynamic_slice_in_dim(tensor, start, STEP_ROWS, 0)
        rows = lax.dynamic_slice_in_dim(runs, start, STEP_ROWS, 0)
        inner_sum = jnp.einsum("ikj,jr->ikr", block, bins_low, preferred_element_type=jnp.float32)
        return total + jnp.einsum("ir,ikr->kr", rows, inner_sum, precision=HIGH)

    local = sweep(step, jnp.zeros((tensor.shape[1], bins.shape[1]), jnp.float32))
    time_terms = lax.psum(local, "runs")
    times = times * time_terms / jnp.dot(times, run_gram * bin_gram, precision=HIGH)
    time_gram = time_gram_sum(times)
    times_low = times.astype(jnp.bfloat16)

    def step(start, total):
        block = lax.dynamic_slice_in_dim(tensor, start, STEP_ROWS, 0)
        rows = lax.dynamic_slice_in_dim(runs, start, STEP_ROWS, 0)
        partial_value = jnp.einsum(
            "ikj,kr->ijr", block, times_low, preferred_element_type=jnp.float32
        )
        return total + jnp.einsum("ir,ijr->jr", rows, partial_value, precision=HIGH)

    local_terms = sweep(step, jnp.zeros((tensor.shape[2], times.shape[1]), jnp.float32))
    mixing = run_gram * time_gram
    bin_terms = lax.psum(local_terms, ("runs", "tm"))
    bins = bins * bin_terms / jnp.dot(bins, mixing, precision=HIGH)
    bin_gram = gram(bins)
    run_bins_low = bins.astype(jnp.bfloat16)

    def step(start, total):
        block = lax.dynamic_slice_in_dim(tensor, start, STEP_ROWS, 0)
        inner_sum = jnp.einsum(
            "ikj,jr->ikr", block, run_bins_low, preferred_element_type=jnp.float32
        )
        row_terms = jnp.einsum("kr,ikr->ir", times, inner_sum, precision=HIGH)
        return lax.dynamic_update_slice_in_dim(total, row_terms, start, 0)

    local = sweep(step, jnp.zeros((rowcap, bins.shape[1]), jnp.float32))
    run_terms = lax.psum(local, "tm")
    runs = runs * run_terms / (jnp.dot(runs, bin_gram * time_gram, precision=HIGH) + 1.0 - live)
    return (runs, bins, times)


def solution(mesh):
    return jax.shard_map(
        shards,
        mesh=mesh,
        in_specs=(P("runs", "tm", None), P("runs"), P("runs", None), P(), P("tm", None)),
        out_specs=(P("runs", None), P(), P("tm", None)),
        check_vma=False,
    )
```

profile of v0, /device:TPU:1, one launch (start us, length us, event | category | flops | bytes accessed | tf_op | source)
XLA Modules:
  0.0 287.8 jit_solution(1251265957969383238)
XLA Ops:
  7.9 0.8 broadcast_multiply_fusion
  8.7 0.9 fusion.20
  9.7 1.1 convert_element_type.17
  10.8 0.3 while.30
  10.9 0.2 fusion.45
  11.1 36.1 %psum.35 = f32[16,128]{1,0:T(8,128)S(1)} all-reduce(f32[16,128]{1,0:T(8,128)S(1)} %get-tuple-element.102), channel_id=1, replica_groups=mesh['runs'=16,'tm'=2] {'runs'}, use_global_device_ids=true, to_apply=%region_2.3 | all-reduce | flops 2048 | bytes 16384 | tf_op jit(solution)/shard_map/psum | solution.py:46
  47.3 69.0 %all-reduce.4.cloned.1.call-done = f32[128,128]{1,0:T(8,128)} async-done(((f32[128,128]{1,0:T(8,128)}), f32[128,128]{1,0:T(8,128)}) %all-reduce.4.cloned.1.call-update) | async-done | bytes 65552 | tf_op jit(solution)/shard_map/psum | solution.py:15
  116.3 1.8 convolution_multiply_fusion.1
  118.1 0.2 fusion.18
  118.3 0.9 fusion.21
  119.4 1.0 while.31
  119.4 0.8 multiply_reduce_fusion.2
  120.3 1.0 copy.8
  121.3 0.2 copy.9
  121.5 16.9 %all-reduce.8.cloned.1.call-done = f32[128,128]{1,0:T(8,128)} async-done(((f32[128,128]{1,0:T(8,128)}), f32[128,128]{1,0:T(8,128)}) %all-reduce.8.cloned.1.call-update) | async-done | bytes 65552 | tf_op jit(solution)/shard_map/psum | solution.py:19
  138.4 134.5 %all-reduce.6.cloned.1.call-done = f32[1024,128]{0,1:T(8,128)} async-done(((f32[1024,128]{0,1:T(8,128)}), f32[1024,128]{0,1:T(8,128)}) %all-reduce.6.cloned.1.call-update) | async-done | bytes 524304 | tf_op jit(solution)/shard_map/psum | solution.py:61
  273.0 1.7 fusion.19
  274.7 1.0 copy.11
  275.7 0.2 copy.10
  275.9 0.3 while.32
  275.9 0.2 fusion.50
  276.2 3.7 %psum.39 = f32[16,128]{1,0:T(8,128)S(1)} all-reduce(f32[16,128]{1,0:T(8,128)S(1)} %get-tuple-element.104), channel_id=1, replica_groups=mesh['runs'=16,'tm'=2] {'tm'}, use_global_device_ids=true, to_apply=%region_10.11 | all-reduce | flops 2048 | bytes 16384 | tf_op jit(solution)/shard_map/psum | solution.py:75
  279.9 0.6 convolution_multiply_fusion
  280.5 0.8 fusion.15
  (27 shorter events, 0.4 us)
Async XLA Ops:
  7.2 3.7 %copy-start = (bf16[16,16,1024]{2,1,0:T(8,128)(2,1)S(1)}, bf16[16,16,1024]{2,1,0:T(8,128)(2,1)}, u32[]{:S(2)}) copy-start(bf16[16,16,1024]{2,1,0:T(8,128)(2,1)} %param.11) | copy-start | bytes 1572868
  7.2 109.1 %all-reduce.4.cloned.1.call-start = ((), (), s32[]{:S(2)}) async-start(), calls=%async_computation | async-start | bytes 131072 | tf_op jit(solution)/shard_map/psum | solution.py:15
  9.6 128.8 %all-reduce.8.cloned.1.call-start = ((), (), s32[]{:S(2)}) async-start(), calls=%async_computation.2 | async-start | bytes 131072 | tf_op jit(solution)/shard_map/psum | solution.py:19
  10.8 105.5 %copy-start.1 = (f32[1024,128]{1,0:T(8,128)S(1)}, f32[1024,128]{1,0:T(8,128)}, u32[]{:S(2)}) copy-start(f32[1024,128]{1,0:T(8,128)} %param.14) | copy-start | bytes 1572868
  47.3 70.9 %copy-start.5 = (f32[16,128]{1,0:T(8,128)S(1)}, f32[16,128]{1,0:T(8,128)}, u32[]{:S(2)}) copy-start(f32[16,128]{1,0:T(8,128)} %param.15) | copy-start | bytes 24580
  119.3 153.7 %all-reduce.6.cloned.1.call-start = ((), (), s32[]{:S(2)}) async-start(), calls=%async_computation.1 | async-start | bytes 1048576 | tf_op jit(solution)/shard_map/psum | solution.py:61
  121.3 151.6 %copy-start.3 = (f32[128,128]{1,0:T(8,128)S(1)}, f32[128,128]{1,0:T(8,128)}, u32[]{:S(2)}) copy-start(f32[128,128]{1,0:T(8,128)} %all-reduce.4.cloned.1.call-done) | copy-start | bytes 196612
  275.9 4.0 %copy-start.4 = (f32[128,128]{1,0:T(8,128)S(1)}, f32[128,128]{1,0:T(8,128)}, u32[]{:S(2)}) copy-start(f32[128,128]{1,0:T(8,128)} %all-reduce.8.cloned.1.call-done) | copy-start | bytes 196612
  276.2 4.3 %copy-start.2 = (f32[16,128]{1,0:T(8,128)}, f32[16,128]{1,0:T(8,128)S(1)}, u32[]{:S(2)}) copy-start(f32[16,128]{1,0:T(8,128)S(1)} %get-tuple-element.367) | copy-start | bytes 24580
Sparse Core Ops, SparseCore 0:
  14.1 102.1 all-reduce.3
  119.4 19.0 all-reduce.7
  145.1 127.7 all-reduce.5
where the time goes:
time: 288 us
  waiting for transfers between devices  220 us (76%)
  blocking collectives  39.8 us (14%)
  between operations  14.7 us (5%)
  matrix products  8.18 us (3%)
    psum x1, waiting for transfers between devices, shards(): bin_terms = lax.psum(local_terms, ('runs', 'tm'))  135 us
    psum x1, waiting for transfers between devices, run_gram_sum(): return lax.psum(gram(runs), 'runs')  69 us
    psum x1, blocking collectives, shards(): time_terms = lax.psum(local, 'runs')  36.1 us
    psum x1, waiting for transfers between devices, time_gram_sum(): return lax.psum(gram(times), 'tm')  16.9 us
  transfers between devices with their start and end apart: 3, of which 3 were waited for; matrix products, arithmetic and copies ran while one was open for 1% of the time, Pallas kernels for 0%

commit v1 on v0

v1 whole, which is shorter than its diff:
```python
import functools

import jax
import jax.numpy as jnp
from jax import lax
from jax.experimental import pallas as pl
from jax.experimental.pallas import tpu as pltpu
from jax.sharding import PartitionSpec as P

HIGH = lax.Precision.HIGHEST
STEP_ROWS = 8
MESH = pl.DeviceIdType.MESH
F32 = jnp.float32
BF16 = jnp.bfloat16


def gram(factor):
    return jnp.dot(factor.T, factor, precision=HIGH)


def run_gram_sum(runs):
    return lax.psum(gram(runs), "runs")


def time_gram_sum(times):
    return lax.psum(gram(times), "tm")


def shards(tensor, run_counts, run_init, bin_init, time_init):
    rowcap = tensor.shape[0]
    count = run_counts[0]
    live = (jnp.arange(rowcap, dtype=jnp.int32) < count).astype(F32)[:, None]
    blocks = (count + STEP_ROWS - 1) // STEP_ROWS
    runs = run_init * live
    bins = bin_init
    times = time_init

    def sweep(step, init):
        return lax.fori_loop(0, blocks, lambda index, carry: step(index * STEP_ROWS, carry), init)

    run_gram = run_gram_sum(runs)
    bin_gram = gram(bins)
    bins_low = bins.astype(BF16)

    def step(start, total):
        block = lax.dynamic_slice_in_dim(tensor, start, STEP_ROWS, 0)
        rows = lax.dynamic_slice_in_dim(runs, start, STEP_ROWS, 0)
        inner_sum = jnp.einsum("ikj,jr->ikr", block, bins_low, preferred_element_type=F32)
        return total + jnp.einsum("ir,ikr->kr", rows, inner_sum, precision=HIGH)

    local = sweep(step, jnp.zeros((tensor.shape[1], bins.shape[1]), F32))
    time_terms = lax.psum(local, "runs")
    times = times * time_terms / jnp.dot(times, run_gram * bin_gram, precision=HIGH)
    time_gram = time_gram_sum(times)
    times_low = times.astype(BF16)

    def step(start, total):
        block = lax.dynamic_slice_in_dim(tensor, start, STEP_ROWS, 0)
        rows = lax.dynamic_slice_in_dim(runs, start, STEP_ROWS, 0)
        partial_value = jnp.einsum("ikj,kr->ijr", block, times_low, preferred_element_type=F32)
        return total + jnp.einsum("ir,ijr->jr", rows, partial_value, precision=HIGH)

    local_terms = sweep(step, jnp.zeros((tensor.shape[2], times.shape[1]), F32))
    mixing = run_gram * time_gram
    bin_terms = lax.psum(local_terms, ("runs", "tm"))
    bins = bins * bin_terms / jnp.dot(bins, mixing, precision=HIGH)
    bin_gram = gram(bins)
    run_bins_low = bins.astype(BF16)

    def step(start, total):
        block = lax.dynamic_slice_in_dim(tensor, start, STEP_ROWS, 0)
        inner_sum = jnp.einsum("ikj,jr->ikr", block, run_bins_low, preferred_element_type=F32)
        row_terms = jnp.einsum("kr,ikr->ir", times, inner_sum, precision=HIGH)
        return lax.dynamic_update_slice_in_dim(total, row_terms, start, 0)

    local = sweep(step, jnp.zeros((rowcap, bins.shape[1]), F32))
    run_terms = lax.psum(local, "tm")
    runs = runs * run_terms / (jnp.dot(runs, bin_gram * time_gram, precision=HIGH) + 1.0 - live)
    return (runs, bins, times)


def dot_t(a, b):
    return lax.dot_general(
        a, b, (((0,), (0,)), ((), ())), precision=HIGH, preferred_element_type=F32
    )


def dot_f32(a, b):
    return lax.dot_general(
        a, b, (((1,), (0,)), ((), ())), precision=HIGH, preferred_element_type=F32
    )


def dot_low(a, b):
    return lax.dot_general(a, b, (((1,), (0,)), ((), ())), preferred_element_type=F32)


def split(x):
    hi = x.astype(BF16)
    return hi, (x - hi.astype(F32)).astype(BF16)


def kernel(
    n, m, count_ref, tensor_ref, run_ref, bin_ref, time_ref,
    run_out, bin_out, time_out,
    wide, wide_in, flipped, terms, terms_in, bins_all, halves, parts, parts_in,
    times_all, times_flat,
    wide_s, wide_r, half_s, half_r, fwd_s, fwd_r, part_s, part_r, row_s, row_r,
    term_s, term_r, bin_s, bin_r, pass_s, pass_r, out_sem,
):
    me = lax.axis_index("runs")
    tm = lax.axis_index("tm")
    rows = run_ref.shape[0]
    kk = time_ref.shape[0]
    jj, rank = bin_ref.shape
    block = jj // (n * m)
    half = rows // m
    span = jj // m
    flat = tm * n + me

    def copy(src, dst, send, recv, run_index, tm_index):
        made = pltpu.make_async_remote_copy(
            src_ref=src, dst_ref=dst, send_sem=send, recv_sem=recv,
            device_id=(run_index, tm_index), device_id_type=MESH,
        )
        made.start()
        return made

    barrier = pltpu.get_barrier_semaphore()
    for off in range(1, n * m):
        peer = lax.rem(flat + off, n * m)
        pl.semaphore_signal(
            barrier, inc=1, device_id=(lax.rem(peer, n), peer // n), device_id_type=MESH
        )

    live = (lax.broadcasted_iota(jnp.int32, (rows, rank), 0) < count_ref[0]).astype(F32)
    runs = run_ref[...] * live
    halves[flat] = jnp.where(tm == 0, runs[:half], runs[rows - half:]) if m == 2 else runs
    tensor = tensor_ref[...]
    wide[...] = tensor.astype(F32)
    times = time_ref[...]
    inner = dot_low(tensor, bin_ref[...].astype(BF16)).reshape(rows, kk, rank)
    upper = inner[0] * runs[0:1]
    for i in range(1, rows):
        upper = upper + inner[i] * runs[i:i + 1]
    lower = dot_f32(times, dot_t(runs, runs) * dot_t(bin_ref[...], bin_ref[...]))
    both = jnp.concatenate([upper, lower], axis=1)
    for k in range(kk):
        parts[k] = both[k:k + 1]

    pl.semaphore_wait(barrier, n * m - 1)

    part_copies = []
    for off in range(1, n):
        peer = lax.rem(me + off, n)
        part_copies.append(
            copy(parts.at[peer], parts_in.at[off], part_s.at[off], part_r.at[off], peer, tm)
        )
    wide_copies = []
    for off in range(1, m):
        peer = lax.rem(tm + off, m)
        wide_copies.append(
            copy(wide, wide_in.at[off], wide_s.at[off], wide_r.at[off], me, peer)
        )
    half_copies = []
    for off in range(1, n):
        peer = lax.rem(me + off, n)
        half_copies.append(
            copy(halves.at[flat], halves.at[flat], half_s.at[off], half_r.at[off], peer, tm)
        )

    start = pl.multiple_of(tm * span, span)
    flipped[:, : rows * kk] = wide[:, pl.ds(start, span)].T.astype(BF16)

    total = parts[me]
    for made, off in zip(part_copies, range(1, n)):
        made.wait_recv()
        total = total + parts_in[off]
    times_all[flat] = time_ref[pl.ds(me, 1), :] * total[:, :rank] / total[:, rank:]
    row_copies = []
    for off in range(1, n * m):
        peer = lax.rem(flat + off, n * m)
        row_copies.append(
            copy(
                times_all.at[flat], times_all.at[flat], row_s.at[off], row_r.at[off],
                lax.rem(peer, n), peer // n,
            )
        )
    for made in half_copies:
        made.wait_recv()
    fwd_copies = []
    mine = pl.ds(tm * n, n)
    for off in range(1, m):
        peer = lax.rem(tm + off, m)
        fwd_copies.append(
            copy(halves.at[mine], halves.at[mine], fwd_s.at[off], fwd_r.at[off], me, peer)
        )
    for off in range(1, m):
        wide_copies[off - 1].wait_recv()
        flipped[:, off * rows * kk:(off + 1) * rows * kk] = (
            wide_in[off, :, pl.ds(start, span)].T.astype(BF16)
        )
    for made in fwd_copies:
        made.wait_recv()
    every = halves[...].reshape(n * m * half, rank)
    run_gram = dot_t(every, every)
    for made in row_copies:
        made.wait_recv()
    for k in range(n * m):
        times_flat[k:k + 1, :] = times_all[k]

    weights = []
    for off in range(m):
        index = lax.rem(tm + off, m)
        low = times_flat[pl.ds(pl.multiple_of(index * kk, kk), kk), :].astype(BF16).astype(F32)
        weights.extend(low * runs[i:i + 1] for i in range(rows))
    hi, lo = split(jnp.concatenate(weights, axis=0))
    product = dot_low(flipped[...], jnp.concatenate([hi, lo], axis=1))
    terms[...] = (product[:, :rank] + product[:, rank:]).reshape(n, block, rank)
    term_copies = []
    for off in range(1, n):
        peer = lax.rem(me + off, n)
        term_copies.append(
            copy(terms.at[peer], terms_in.at[off], term_s.at[off], term_r.at[off], peer, tm)
        )
    every_time = times_flat[...]
    time_gram = dot_t(every_time, every_time)
    own = bin_ref[pl.ds(pl.multiple_of(flat * block, block), block), :]
    scale = own / dot_f32(own, run_gram * time_gram)
    total = terms[me]
    for made, off in zip(term_copies, range(1, n)):
        made.wait_recv()
        total = total + terms_in[off]
    bins_all[flat] = scale * total

    bin_copies = []
    for off in range(1, n):
        peer = lax.rem(me + off, n)
        bin_copies.append(
            copy(bins_all.at[flat], bins_all.at[flat], bin_s.at[off], bin_r.at[off], peer, tm)
        )
    pass_copies = []
    for step in range(n):
        if step > 0:
            bin_copies[step - 1].wait_recv()
        source = tm * n + lax.rem(me - step + n, n)
        for off in range(1, m):
            peer = lax.rem(tm + off, m)
            pass_copies.append(
                copy(
                    bins_all.at[source], bins_all.at[source],
                    pass_s.at[step, off], pass_r.at[step, off], me, peer,
                )
            )
    for made in pass_copies:
        made.wait_recv()
    write = pltpu.make_async_copy(bins_all, bin_out, out_sem)
    write.start()
    bins = bins_all[...].reshape(jj, rank)
    bins_low = bins.astype(BF16)
    run_terms = None
    for off in range(m):
        index = lax.rem(tm + off, m)
        slab = tensor_ref[...] if off == 0 else wide_in[off].astype(BF16)
        inner = dot_low(slab, bins_low).reshape(rows, kk, rank)
        weight = times_flat[pl.ds(pl.multiple_of(index * kk, kk), kk), :]
        some = jnp.sum(inner * weight[None], axis=1)
        run_terms = some if run_terms is None else run_terms + some
    mixing = dot_t(bins, bins) * time_gram
    run_out[...] = runs * run_terms / (dot_f32(runs, mixing) + 1.0 - live)
    time_out[...] = times_flat[pl.ds(pl.multiple_of(tm * kk, kk), kk), :]

    for made in (
        part_copies + wide_copies + half_copies + row_copies + fwd_copies
        + term_copies + bin_copies + pass_copies
    ):
        made.wait_send()
    write.wait()


def fused(n, m, tensor, run_counts, run_init, bin_init, time_init):
    rows, kk, jj = tensor.shape
    rank = bin_init.shape[1]
    block = jj // (n * m)
    half = rows // m
    dma = pltpu.SemaphoreType.DMA
    vmem = pl.BlockSpec(memory_space=pltpu.VMEM)
    runs, bins, times = pl.pallas_call(
        functools.partial(kernel, n, m),
        out_shape=(
            jax.ShapeDtypeStruct((rows, rank), F32),
            jax.ShapeDtypeStruct((n * m, block, rank), F32),
            jax.ShapeDtypeStruct((kk, rank), F32),
        ),
        in_specs=[pl.BlockSpec(memory_space=pltpu.SMEM)] + [vmem] * 4,
        out_specs=(vmem, pl.BlockSpec(memory_space=pl.ANY), vmem),
        scratch_shapes=[
            pltpu.VMEM((rows * kk, jj), F32),
            pltpu.VMEM((m, rows * kk, jj), F32),
            pltpu.VMEM((jj // m, m * rows * kk), BF16),
            pltpu.VMEM((n, block, rank), F32),
            pltpu.VMEM((n, block, rank), F32),
            pltpu.VMEM((n * m, block, rank), F32),
            pltpu.VMEM((n * m, half, rank), F32),
            pltpu.VMEM((n, 1, 2 * rank), F32),
            pltpu.VMEM((n, 1, 2 * rank), F32),
            pltpu.VMEM((n * m, 1, rank), F32),
            pltpu.VMEM((n * m, rank), F32),
            dma((m,)), dma((m,)), dma((n,)), dma((n,)), dma((m,)), dma((m,)),
            dma((n,)), dma((n,)), dma((n * m,)), dma((n * m,)),
            dma((n,)), dma((n,)), dma((n,)), dma((n,)), dma((n, m)), dma((n, m)), dma,
        ],
        compiler_params=pltpu.CompilerParams(
            collective_id=0, has_side_effects=True, vmem_limit_bytes=40 * 2**20
        ),
    )(run_counts, tensor.reshape(rows * kk, jj), run_init, bin_init, time_init)
    return runs, bins.reshape(jj, rank), times


def update(n, m, *args):
    rows, kk, jj = args[0].shape
    fits = m == 2 and kk == n and kk % 16 == 0 and rows % (8 * m) == 0 and jj % (8 * n * m) == 0
    return fused(n, m, *args) if fits else shards(*args)


def solution(mesh):
    return jax.shard_map(
        functools.partial(update, mesh.shape["runs"], mesh.shape["tm"]),
        mesh=mesh,
        in_specs=(P("runs", "tm", None), P("runs"), P("runs", None), P(), P("tm", None)),
        out_specs=(P("runs", None), P(), P("tm", None)),
        check_vma=False,
    )
```

time: 288 us -> 41.1 us (0.14)
  waiting for transfers between devices: 220 us -> 0 us
  blocking collectives: 39.8 us -> 0 us
  Pallas kernels: 0 us -> 34.1 us
  between operations: 14.7 us -> 1.3 us
  matrix products: 8.18 us -> 0 us
  local copies, waits for them, and re-layouts: 2.45 us -> 5.46 us
    psum x3 -> x0, waiting for transfers between devices: 220 us -> none  [the longest x1 135 us: shards(): bin_terms = lax.psum(local_terms, ('runs', 'tm'))]
    psum x2 -> x0, blocking collectives: 39.8 us -> none  [the longest x1 36.1 us: shards(): time_terms = lax.psum(local, 'runs')]
    pallas_call x0 -> x1, Pallas kernels: none -> 34.1 us  [fused(): pl.pallas_call(functools.partial(kernel, n, m), out_shape=(jax.ShapeDtype...]
    dot_general x10 -> x0, matrix products: 8.18 us -> none  [the longest x4 4.27 us: gram(): return jnp.dot(factor.T, factor, precision=HIGH)]
    unnamed x14 -> x11, local copies, waits for them, and re-layouts: 1.22 us -> 5.46 us
  transfers between devices with their start and end apart: 3 -> 0, of which waited for: 3 -> 0; matrix products, arithmetic and copies ran while one was open for 1% -> 0% of each run, Pallas kernels for 0% -> 0%
where the time goes in v1:
time: 41.1 us; the launch traced here: 40.8 us
  Pallas kernels  34.1 us (83%)
  local copies, waits for them, and re-layouts  5.46 us (13%)
  between operations  1.3 us (3%)
    pallas_call x1, Pallas kernels, fused(): pl.pallas_call(functools.partial(kernel, n, m), out_shape=(jax.ShapeDtype...  34.1 us
    unnamed x11, local copies, waits for them, and re-layouts  5.46 us

profile of v1, /device:TPU:1, one launch (start us, length us, event | category | flops | bytes accessed | tf_op | source)
XLA Modules:
  0.0 40.8 jit_solution(14505245804433369574)
XLA Ops:
  1.3 0.0 copy-start
  1.3 1.0 %copy-done = bf16[16,16,1024]{2,1,0:T(8,128)(2,1)S(1)} copy-done((bf16[16,16,1024]{2,1,0:T(8,128)(2,1)S(1)}, bf16[16,16,1024]{2,1,0:T(8,128)(2,1)}, u32[]{:S(2)}) %copy-start) | copy-done | bytes 524312
  2.3 0.0 copy-start.1
  2.3 1.0 %copy-done.1 = f32[1024,128]{1,0:T(8,128)S(1)} copy-done((f32[1024,128]{1,0:T(8,128)S(1)}, f32[1024,128]{1,0:T(8,128)}, u32[]{:S(2)}) %copy-start.1) | copy-done | bytes 524312
  3.4 0.0 copy-start.2
  3.4 0.7 %copy-done.2 = f32[16,128]{1,0:T(8,128)S(1)} copy-done((f32[16,128]{1,0:T(8,128)S(1)}, f32[16,128]{1,0:T(8,128)}, u32[]{:S(2)}) %copy-start.2) | copy-done | bytes 8216
  4.1 0.0 copy-start.3
  4.1 0.7 %copy-done.3 = f32[16,128]{1,0:T(8,128)S(1)} copy-done((f32[16,128]{1,0:T(8,128)S(1)}, f32[16,128]{1,0:T(8,128)}, u32[]{:S(2)}) %copy-start.3) | copy-done | bytes 8216
  4.8 34.1 %shard_map.76 = (f32[16,128]{1,0:T(8,128)S(1)}, f32[32,32,128]{2,1,0:T(8,128)S(1)}, f32[16,128]{1,0:T(8,128)S(1)}) custom-call(s32[1]{0:T(128)S(6)} %copy.11.count_ref, bf16[256,1024]{1,0:T(8,128)(2,1)S(1)} %bitcast.3, f32[16,128]{1,0:T(8,128)S(1)} %copy-done.2, f32[1024,128]{1,0:T(8,128)S(1)} %copy-done.1, f32[16,128]{1,0:T(8,128)S(1)} %copy-done.3), custom_call_target="tpu_custom_call" | custom-call | tf_op jit(solution)/shard_map/pallas_call | solution.py:288
  38.8 0.6 %copy.12 = f32[16,128]{1,0:T(8,128)} copy(f32[16,128]{1,0:T(8,128)S(1)} %get-tuple-element.12) | data formatting | bytes 16384
  39.4 0.8 %copy.13 = f32[1024,128]{1,0:T(8,128)} copy(f32[1024,128]{1,0:T(8,128)S(1)} %bitcast.2) | data formatting | bytes 1048576
  40.2 0.6 %copy.14 = f32[16,128]{1,0:T(8,128)} copy(f32[16,128]{1,0:T(8,128)S(1)} %get-tuple-element.14) | data formatting | bytes 16384
Async XLA Ops:
  1.3 1.0 %copy-start = (bf16[16,16,1024]{2,1,0:T(8,128)(2,1)S(1)}, bf16[16,16,1024]{2,1,0:T(8,128)(2,1)}, u32[]{:S(2)}) copy-start(bf16[16,16,1024]{2,1,0:T(8,128)(2,1)} %param.5) | copy-start | bytes 1572868
  2.3 1.0 %copy-start.1 = (f32[1024,128]{1,0:T(8,128)S(1)}, f32[1024,128]{1,0:T(8,128)}, u32[]{:S(2)}) copy-start(f32[1024,128]{1,0:T(8,128)} %bin_ref.1) | copy-start | bytes 1572868
  3.4 0.7 %copy-start.2 = (f32[16,128]{1,0:T(8,128)S(1)}, f32[16,128]{1,0:T(8,128)}, u32[]{:S(2)}) copy-start(f32[16,128]{1,0:T(8,128)} %run_ref.1) | copy-start | bytes 24580
  4.1 0.7 %copy-start.3 = (f32[16,128]{1,0:T(8,128)S(1)}, f32[16,128]{1,0:T(8,128)}, u32[]{:S(2)}) copy-start(f32[16,128]{1,0:T(8,128)} %time_ref.1) | copy-start | bytes 24580

commit v2 on v1

--- a/solution.py
+++ b/solution.py
@@ -79,34 +79,49 @@
     return (runs, bins, times)
 
 
-def dot_t(a, b):
-    return lax.dot_general(
-        a, b, (((0,), (0,)), ((), ())), precision=HIGH, preferred_element_type=F32
-    )
-
-
-def dot_f32(a, b):
-    return lax.dot_general(
-        a, b, (((1,), (0,)), ((), ())), precision=HIGH, preferred_element_type=F32
-    )
-
-
-def dot_low(a, b):
-    return lax.dot_general(a, b, (((1,), (0,)), ((), ())), preferred_element_type=F32)
-
-
 def split(x):
     hi = x.astype(BF16)
     return hi, (x - hi.astype(F32)).astype(BF16)
 
 
+def dot_low(a, b):
+    return lax.dot_general(a, b, (((1,), (0,)), ((), ())), preferred_element_type=F32)
+
+
+def fold(x):
+    half = x.shape[1] // 2
+    return x[:, :half] + x[:, half:]
+
+
+def self_gram(x):
+    both = jnp.concatenate(split(x), axis=1)
+    product = fold(
+        lax.dot_general(both, both, (((0,), (0,)), ((), ())), preferred_element_type=F32)
+    )
+    half = product.shape[0] // 2
+    return product[:half] + product[half:]
+
+
+def dot_f32(a, b):
+    right = jnp.concatenate(split(b), axis=1)
+    return fold(
+        dot_low(jnp.concatenate(split(a), axis=1), jnp.concatenate([right, right], axis=0))
+    )
+
+
+QUAD = 4
+VMEM_LIMIT = 64 * 2**20 - 2**16
+
+
 def kernel(
-    n, m, count_ref, tensor_ref, run_ref, bin_ref, time_ref,
+    n, m, count_in, tensor_in, run_in, bin_in, time_in,
     run_out, bin_out, time_out,
-    wide, wide_in, flipped, terms, terms_in, bins_all, halves, parts, parts_in,
-    times_all, times_flat,
-    wide_s, wide_r, half_s, half_r, fwd_s, fwd_r, part_s, part_r, row_s, row_r,
-    term_s, term_r, bin_s, bin_r, pass_s, pass_r, out_sem,
+    count_ref, slabs, run_ref, bin_ref, time_ref,
+    wide, wide_in, flipped, terms, terms_one, terms_mid, terms_two, terms_last, terms_three,
+    bins_all, inner_sum, halves, parts, parts_in, times_all, times_flat,
+    load_sem, wide_s, wide_r, half_s, half_r, fwd_s, fwd_r, part_s, part_r, row_s, row_r,
+    one_s, one_r, two_s, two_r, three_s, three_r,
+    z_s, z_r, near_s, near_r, far_s, far_r, pass_s, pass_r, out_sem,
 ):
     me = lax.axis_index("runs")
     tm = lax.axis_index("tm")
@@ -117,6 +132,21 @@
     half = rows // m
     span = jj // m
     flat = tm * n + me
+    zs = n // QUAD
+    strip = QUAD * block
+
+    z = me // QUAD
+    first = 2 - tm
+    second = 1 + tm
+    bit_one = lax.rem(me // first, 2)
+    bit_two = lax.rem(me // second, 2)
+    partner_one = me + first * (1 - 2 * bit_one)
+    partner_two = me + second * (1 - 2 * bit_two)
+
+    def place(z_index, flip_one, flip_two):
+        one = 1 - bit_one if flip_one else bit_one
+        two = 1 - bit_two if flip_two else bit_two
+        return z_index * QUAD + one * first + two * second
 
     def copy(src, dst, send, recv, run_index, tm_index):
         made = pltpu.make_async_remote_copy(
@@ -125,6 +155,16 @@
         )
         made.start()
         return made
+
+    loads = [
+        pltpu.make_async_copy(src, dst, load_sem.at[index])
+        for index, (src, dst) in enumerate((
+            (tensor_in, slabs.at[0]), (bin_in, bin_ref), (count_in, count_ref),
+            (run_in, run_ref), (time_in, time_ref),
+        ))
+    ]
+    for made in loads:
+        made.start()
 
     barrier = pltpu.get_barrier_semaphore()
     for off in range(1, n * m):
@@ -132,18 +172,19 @@
         pl.semaphore_signal(
             barrier, inc=1, device_id=(lax.rem(peer, n), peer // n), device_id_type=MESH
         )
+    for made in loads:
+        made.wait()
 
     live = (lax.broadcasted_iota(jnp.int32, (rows, rank), 0) < count_ref[0]).astype(F32)
     runs = run_ref[...] * live
-    halves[flat] = jnp.where(tm == 0, runs[:half], runs[rows - half:]) if m == 2 else runs
-    tensor = tensor_ref[...]
-    wide[...] = tensor.astype(F32)
+    halves[flat] = jnp.where(tm == 0, runs[:half], runs[rows - half:])
+    tensor = slabs[0]
     times = time_ref[...]
     inner = dot_low(tensor, bin_ref[...].astype(BF16)).reshape(rows, kk, rank)
     upper = inner[0] * runs[0:1]
     for i in range(1, rows):
         upper = upper + inner[i] * runs[i:i + 1]
-    lower = dot_f32(times, dot_t(runs, runs) * dot_t(bin_ref[...], bin_ref[...]))
+    lower = dot_f32(times, self_gram(runs) * self_gram(bin_ref[...]))
     both = jnp.concatenate([upper, lower], axis=1)
     for k in range(kk):
         parts[k] = both[k:k + 1]
@@ -156,6 +197,7 @@
         part_copies.append(
             copy(parts.at[peer], parts_in.at[off], part_s.at[off], part_r.at[off], peer, tm)
         )
+    wide[...] = tensor.astype(F32)
     wide_copies = []
     for off in range(1, m):
         peer = lax.rem(tm + off, m)
@@ -197,13 +239,10 @@
         )
     for off in range(1, m):
         wide_copies[off - 1].wait_recv()
+        slabs[off] = wide_in[off].astype(BF16)
         flipped[:, off * rows * kk:(off + 1) * rows * kk] = (
             wide_in[off, :, pl.ds(start, span)].T.astype(BF16)
         )
-    for made in fwd_copies:
-        made.wait_recv()
-    every = halves[...].reshape(n * m * half, rank)
-    run_gram = dot_t(every, every)
     for made in row_copies:
         made.wait_recv()
     for k in range(n * m):
@@ -214,68 +253,140 @@
         index = lax.rem(tm + off, m)
         low = times_flat[pl.ds(pl.multiple_of(index * kk, kk), kk), :].astype(BF16).astype(F32)
         weights.extend(low * runs[i:i + 1] for i in range(rows))
-    hi, lo = split(jnp.concatenate(weights, axis=0))
-    product = dot_low(flipped[...], jnp.concatenate([hi, lo], axis=1))
-    terms[...] = (product[:, :rank] + product[:, rank:]).reshape(n, block, rank)
-    term_copies = []
-    for off in range(1, n):
-        peer = lax.rem(me + off, n)
-        term_copies.append(
-            copy(terms.at[peer], terms_in.at[off], term_s.at[off], term_r.at[off], peer, tm)
-        )
-    every_time = times_flat[...]
-    time_gram = dot_t(every_time, every_time)
+    weight = jnp.concatenate(split(jnp.concatenate(weights, axis=0)), axis=1)
+    order = list(range(1, zs)) + [0]
+    z_of = [lax.rem(z + k, zs) for k in range(zs)]
+    one_copies = {}
+    for k in order:
+        piece = flipped[pl.ds(pl.multiple_of(z_of[k] * strip, strip), strip), :]
+        terms[pl.ds(z_of[k] * QUAD, QUAD)] = fold(dot_low(piece, weight)).reshape(
+            QUAD, block, rank
+        )
+        for flip in (1, 0):
+            one_copies[k, flip] = copy(
+                terms.at[place(z_of[k], 1, flip)], terms_one.at[k, flip],
+                one_s.at[k, flip], one_r.at[k, flip], partner_one, tm,
+            )
+    two_copies = {}
+    for k in order:
+        one_copies[k, 1].wait_recv()
+        terms_mid[k] = terms[place(z_of[k], 0, 1)] + terms_one[k, 1]
+        two_copies[k] = copy(
+            terms_mid.at[k], terms_two.at[k], two_s.at[k], two_r.at[k], partner_two, tm
+        )
+    for made in fwd_copies:
+        made.wait_recv()
+    run_gram = self_gram(halves[...].reshape(n * m * half, rank))
+    time_gram = self_gram(times_flat[...])
     own = bin_ref[pl.ds(pl.multiple_of(flat * block, block), block), :]
     scale = own / dot_f32(own, run_gram * time_gram)
-    total = terms[me]
-    for made, off in zip(term_copies, range(1, n)):
-        made.wait_recv()
-        total = total + terms_in[off]
+    three_copies = {}
+    for k in order:
+        one_copies[k, 0].wait_recv()
+        two_copies[k].wait_recv()
+        terms_last[k] = terms[place(z_of[k], 0, 0)] + terms_one[k, 0] + terms_two[k]
+        if k > 0:
+            three_copies[k] = copy(
+                terms_last.at[k], terms_three.at[k], three_s.at[k], three_r.at[k],
+                place(z_of[k], 0, 0), tm,
+            )
+    total = terms_last[0]
+    for k in range(1, zs):
+        three_copies[k].wait_recv()
+        total = total + terms_three[k]
     bins_all[flat] = scale * total
 
-    bin_copies = []
-    for off in range(1, n):
-        peer = lax.rem(me + off, n)
-        bin_copies.append(
-            copy(bins_all.at[flat], bins_all.at[flat], bin_s.at[off], bin_r.at[off], peer, tm)
-        )
-    pass_copies = []
-    for step in range(n):
-        if step > 0:
-            bin_copies[step - 1].wait_recv()
-        source = tm * n + lax.rem(me - step + n, n)
-        for off in range(1, m):
-            peer = lax.rem(tm + off, m)
-            pass_copies.append(
-                copy(
-                    bins_all.at[source], bins_all.at[source],
-                    pass_s.at[step, off], pass_r.at[step, off], me, peer,
-                )
+    z_copies = {}
+    for k in range(1, zs):
+        z_copies[k] = copy(
+            bins_all.at[flat], bins_all.at[flat], z_s.at[k], z_r.at[k],
+            place(z_of[k], 0, 0), tm,
+        )
+    from_z = [lax.rem(z - k + zs, zs) for k in range(zs)]
+    near_copies, far_copies, pass_copies = {}, {}, {}
+
+    def send_on(store, key, slot, sends, recvs, run_index, tm_index):
+        store[key] = copy(
+            bins_all.at[slot], bins_all.at[slot], sends.at[key], recvs.at[key],
+            run_index, tm_index,
+        )
+
+    other = lax.rem(tm + 1, m)
+    for k in range(zs):
+        if k > 0:
+            z_copies[k].wait_recv()
+        slot = tm * n + place(from_z[k], 0, 0)
+        send_on(near_copies, k, slot, near_s, near_r, partner_two, tm)
+        send_on(far_copies, (k, 0), slot, far_s, far_r, partner_one, tm)
+        send_on(pass_copies, (k, 0), slot, pass_s, pass_r, me, other)
+    for k in range(zs):
+        near_copies[k].wait_recv()
+        slot = tm * n + place(from_z[k], 0, 1)
+        send_on(far_copies, (k, 1), slot, far_s, far_r, partner_one, tm)
+        send_on(pass_copies, (k, 1), slot, pass_s, pass_r, me, other)
+    for k in range(zs):
+        for flip in (0, 1):
+            far_copies[k, flip].wait_recv()
+            slot = tm * n + place(from_z[k], 1, flip)
+            send_on(pass_copies, (k, 2 + flip), slot, pass_s, pass_r, me, other)
+    bin_gram = None
+    writes = []
+    for k in range(zs):
+        for index in range(QUAD):
+            pass_copies[k, index].wait_recv()
+        pieces = []
+        for core in range(m):
+            mine = pl.ds(core * n + from_z[k] * QUAD, QUAD)
+            pieces.append(bins_all[mine].reshape(strip, rank))
+            made = pltpu.make_async_copy(
+                bins_all.at[mine], bin_out.at[mine], out_sem.at[k, core]
             )
-    for made in pass_copies:
-        made.wait_recv()
-    write = pltpu.make_async_copy(bins_all, bin_out, out_sem)
-    write.start()
-    bins = bins_all[...].reshape(jj, rank)
-    bins_low = bins.astype(BF16)
+            made.start()
+            writes.append(made)
+        bins = jnp.concatenate(pieces, axis=0)
+        bins_low = bins.astype(BF16)
+        some = self_gram(bins)
+        bin_gram = some if k == 0 else bin_gram + some
+        for off in range(m):
+            slab = jnp.concatenate(
+                [
+                    slabs[off, :, pl.ds(pl.multiple_of(core * span + from_z[k] * strip, strip), strip)]
+                    for core in range(m)
+                ],
+                axis=1,
+            )
+            product = dot_low(slab, bins_low)
+            inner_sum[off] = product if k == 0 else inner_sum[off] + product
     run_terms = None
     for off in range(m):
         index = lax.rem(tm + off, m)
-        slab = tensor_ref[...] if off == 0 else wide_in[off].astype(BF16)
-        inner = dot_low(slab, bins_low).reshape(rows, kk, rank)
         weight = times_flat[pl.ds(pl.multiple_of(index * kk, kk), kk), :]
-        some = jnp.sum(inner * weight[None], axis=1)
+        some = jnp.sum(inner_sum[off].reshape(rows, kk, rank) * weight[None], axis=1)
         run_terms = some if run_terms is None else run_terms + some
-    mixing = dot_t(bins, bins) * time_gram
-    run_out[...] = runs * run_terms / (dot_f32(runs, mixing) + 1.0 - live)
+    run_out[...] = runs * run_terms / (dot_f32(runs, bin_gram * time_gram) + 1.0 - live)
     time_out[...] = times_flat[pl.ds(pl.multiple_of(tm * kk, kk), kk), :]
 
-    for made in (
-        part_copies + wide_copies + half_copies + row_copies + fwd_copies
-        + term_copies + bin_copies + pass_copies
+    for made in part_copies + wide_copies + half_copies + row_copies + fwd_copies:
+        made.wait_send()
+    for store in (
+        one_copies, two_copies, three_copies, z_copies, near_copies, far_copies, pass_copies
     ):
-        made.wait_send()
-    write.wait()
+        for made in store.values():
+            made.wait_send()
+    for made in writes:
+        made.wait()
+
+
+def hand_out(*refs):
+    count = (len(refs) - 1) // 2
+    sems = refs[-1]
+    copies = [
+        pltpu.make_async_copy(refs[i], refs[count + i], sems.at[i]) for i in range(count)
+    ]
+    for made in copies:
+        made.start()
+    for made in copies:
+        made.wait()
 
 
 def fused(n, m, tensor, run_counts, run_init, bin_init, time_init):
@@ -283,43 +394,67 @@
     rank = bin_init.shape[1]
     block = jj // (n * m)
     half = rows // m
+    zs = n // QUAD
     dma = pltpu.SemaphoreType.DMA
     vmem = pl.BlockSpec(memory_space=pltpu.VMEM)
-    runs, bins, times = pl.pallas_call(
+    anywhere = pl.BlockSpec(memory_space=pl.ANY)
+    shapes = (
+        jax.ShapeDtypeStruct((rows, rank), F32),
+        jax.ShapeDtypeStruct((n * m, block, rank), F32),
+        jax.ShapeDtypeStruct((kk, rank), F32),
+    )
+    results = pl.pallas_call(
         functools.partial(kernel, n, m),
-        out_shape=(
-            jax.ShapeDtypeStruct((rows, rank), F32),
-            jax.ShapeDtypeStruct((n * m, block, rank), F32),
-            jax.ShapeDtypeStruct((kk, rank), F32),
-        ),
-        in_specs=[pl.BlockSpec(memory_space=pltpu.SMEM)] + [vmem] * 4,
-        out_specs=(vmem, pl.BlockSpec(memory_space=pl.ANY), vmem),
+        out_shape=shapes,
+        in_specs=[anywhere] * 5,
+        out_specs=(vmem, anywhere, vmem),
         scratch_shapes=[
+            pltpu.SMEM((1,), jnp.int32),
+            pltpu.VMEM((m, rows * kk, jj), BF16),
+            pltpu.VMEM((rows, rank), F32),
+            pltpu.VMEM((jj, rank), F32),
+            pltpu.VMEM((kk, rank), F32),
             pltpu.VMEM((rows * kk, jj), F32),
             pltpu.VMEM((m, rows * kk, jj), F32),
             pltpu.VMEM((jj // m, m * rows * kk), BF16),
             pltpu.VMEM((n, block, rank), F32),
-            pltpu.VMEM((n, block, rank), F32),
+            pltpu.VMEM((zs, 2, block, rank), F32),
+            pltpu.VMEM((zs, block, rank), F32),
+            pltpu.VMEM((zs, block, rank), F32),
+            pltpu.VMEM((zs, block, rank), F32),
+            pltpu.VMEM((zs, block, rank), F32),
             pltpu.VMEM((n * m, block, rank), F32),
+            pltpu.VMEM((m, rows * kk, rank), F32),
             pltpu.VMEM((n * m, half, rank), F32),
             pltpu.VMEM((n, 1, 2 * rank), F32),
             pltpu.VMEM((n, 1, 2 * rank), F32),
             pltpu.VMEM((n * m, 1, rank), F32),
             pltpu.VMEM((n * m, rank), F32),
-            dma((m,)), dma((m,)), dma((n,)), dma((n,)), dma((m,)), dma((m,)),
+            dma((5,)), dma((m,)), dma((m,)), dma((n,)), dma((n,)), dma((m,)), dma((m,)),
             dma((n,)), dma((n,)), dma((n * m,)), dma((n * m,)),
-            dma((n,)), dma((n,)), dma((n,)), dma((n,)), dma((n, m)), dma((n, m)), dma,
+            dma((zs, 2)), dma((zs, 2)), dma((zs,)), dma((zs,)), dma((zs,)), dma((zs,)),
+            dma((zs,)), dma((zs,)), dma((zs,)), dma((zs,)), dma((zs, 2)), dma((zs, 2)),
+            dma((zs, QUAD)), dma((zs, QUAD)), dma((zs, m)),
         ],
         compiler_params=pltpu.CompilerParams(
-            collective_id=0, has_side_effects=True, vmem_limit_bytes=40 * 2**20
+            collective_id=0, has_side_effects=True, vmem_limit_bytes=VMEM_LIMIT
         ),
     )(run_counts, tensor.reshape(rows * kk, jj), run_init, bin_init, time_init)
+    runs, bins, times = pl.pallas_call(
+        hand_out,
+        out_shape=shapes,
+        in_specs=[anywhere] * 3,
+        out_specs=[anywhere] * 3,
+        scratch_shapes=[dma((3,))],
+        compiler_params=pltpu.CompilerParams(vmem_limit_bytes=VMEM_LIMIT),
+    )(*results)
     return runs, bins.reshape(jj, rank), times
 
 
 def update(n, m, *args):
     rows, kk, jj = args[0].shape
-    fits = m == 2 and kk == n and kk % 16 == 0 and rows % (8 * m) == 0 and jj % (8 * n * m) == 0
+    fits = m == 2 and kk == n and n % QUAD == 0 and kk % 16 == 0 and rows % (8 * m) == 0
+    fits = fits and jj % (8 * n * m) == 0 and (QUAD * jj // (n * m)) % 128 == 0
     return fused(n, m, *args) if fits else shards(*args)
 
 

time: 41.1 us -> 59.3 us (1.44)
  Pallas kernels: 34.1 us -> 57.9 us
  local copies, waits for them, and re-layouts: 5.46 us -> 0 us
    pallas_call x1 -> x2, Pallas kernels: 34.1 us -> 57.9 us  [the longest x1 40.4 us: fused(): pl.pallas_call(functools.partial(kernel, n, m), out_shape=shapes, in_spec...]
    unnamed x11 -> x0, local copies, waits for them, and re-layouts: 5.46 us -> none
where the time goes in v2:
time: 59.3 us; the launch traced here: 59.2 us
  Pallas kernels  57.9 us (98%)
  between operations  1.28 us (2%)
    pallas_call x1, Pallas kernels, fused(): pl.pallas_call(functools.partial(kernel, n, m), out_shape=shapes, in_spec...  40.4 us
    pallas_call x1, Pallas kernels, fused(): pl.pallas_call(hand_out, out_shape=shapes, in_specs=[anywhere] * 3, out_s...  17.5 us

profile of v2, /device:TPU:1, one launch (start us, length us, event | category | flops | bytes accessed | tf_op | source)
XLA Modules:
  0.0 59.2 jit_solution(10682384880760557913)
XLA Ops:
  1.3 40.4 %shard_map.76 = (f32[16,128]{1,0:T(8,128)}, f32[32,32,128]{2,1,0:T(8,128)}, f32[16,128]{1,0:T(8,128)}) custom-call(s32[1]{0:T(128)S(6)} %copy.8.count_in, bf16[256,1024]{1,0:T(8,128)(2,1)} %bitcast.2, f32[16,128]{1,0:T(8,128)} %run_in.1, f32[1024,128]{1,0:T(8,128)} %bin_in.1, f32[16,128]{1,0:T(8,128)} %time_in.1), custom_call_target="tpu_custom_call" | custom-call | tf_op jit(solution)/shard_map/pallas_call | solution.py:406
  41.7 17.5 %shard_map.77 = (f32[16,128]{1,0:T(8,128)}, f32[32,32,128]{2,1,0:T(8,128)}, f32[16,128]{1,0:T(8,128)}) custom-call(f32[16,128]{1,0:T(8,128)} %get-tuple-element.9.refs_0_, f32[32,32,128]{2,1,0:T(8,128)} %get-tuple-element.10.refs_1_, f32[16,128]{1,0:T(8,128)} %get-tuple-element.11.refs_2_), custom_call_target="tpu_custom_call" | custom-call | tf_op jit(solution)/shard_map/pallas_call | solution.py:443

commit v3 on v2

--- a/solution.py
+++ b/solution.py
@@ -117,11 +117,10 @@
     n, m, count_in, tensor_in, run_in, bin_in, time_in,
     run_out, bin_out, time_out,
     count_ref, slabs, run_ref, bin_ref, time_ref,
-    wide, wide_in, flipped, terms, terms_one, terms_mid, terms_two, terms_last, terms_three,
+    wide, wide_in, flipped, terms, terms_in,
     bins_all, inner_sum, halves, parts, parts_in, times_all, times_flat,
     load_sem, wide_s, wide_r, half_s, half_r, fwd_s, fwd_r, part_s, part_r, row_s, row_r,
-    one_s, one_r, two_s, two_r, three_s, three_r,
-    z_s, z_r, near_s, near_r, far_s, far_r, pass_s, pass_r, out_sem,
+    term_s, term_r, bin_s, bin_r, pass_s, pass_r, out_sem,
 ):
     me = lax.axis_index("runs")
     tm = lax.axis_index("tm")
@@ -136,17 +135,14 @@
     strip = QUAD * block
 
     z = me // QUAD
-    first = 2 - tm
-    second = 1 + tm
-    bit_one = lax.rem(me // first, 2)
-    bit_two = lax.rem(me // second, 2)
-    partner_one = me + first * (1 - 2 * bit_one)
-    partner_two = me + second * (1 - 2 * bit_two)
-
-    def place(z_index, flip_one, flip_two):
-        one = 1 - bit_one if flip_one else bit_one
-        two = 1 - bit_two if flip_two else bit_two
-        return z_index * QUAD + one * first + two * second
+    q = lax.rem(me, QUAD)
+    steps = [(k, t) for k in list(range(1, zs)) + [0] for t in range(QUAD) if (k, t) != (0, 0)]
+
+    def ahead(k, t):
+        return lax.rem(z + k, zs) * QUAD + lax.rem(q + t, QUAD)
+
+    def behind(k, t):
+        return lax.rem(z - k + zs, zs) * QUAD + lax.rem(q - t + QUAD, QUAD)
 
     def copy(src, dst, send, recv, run_index, tm_index):
         made = pltpu.make_async_remote_copy(
@@ -254,109 +250,80 @@
         low = times_flat[pl.ds(pl.multiple_of(index * kk, kk), kk), :].astype(BF16).astype(F32)
         weights.extend(low * runs[i:i + 1] for i in range(rows))
     weight = jnp.concatenate(split(jnp.concatenate(weights, axis=0)), axis=1)
-    order = list(range(1, zs)) + [0]
-    z_of = [lax.rem(z + k, zs) for k in range(zs)]
-    one_copies = {}
-    for k in order:
-        piece = flipped[pl.ds(pl.multiple_of(z_of[k] * strip, strip), strip), :]
-        terms[pl.ds(z_of[k] * QUAD, QUAD)] = fold(dot_low(piece, weight)).reshape(
-            QUAD, block, rank
-        )
-        for flip in (1, 0):
-            one_copies[k, flip] = copy(
-                terms.at[place(z_of[k], 1, flip)], terms_one.at[k, flip],
-                one_s.at[k, flip], one_r.at[k, flip], partner_one, tm,
-            )
-    two_copies = {}
-    for k in order:
-        one_copies[k, 1].wait_recv()
-        terms_mid[k] = terms[place(z_of[k], 0, 1)] + terms_one[k, 1]
-        two_copies[k] = copy(
-            terms_mid.at[k], terms_two.at[k], two_s.at[k], two_r.at[k], partner_two, tm
-        )
+    term_copies = {}
+    for k in list(range(1, zs)) + [0]:
+        to_z = lax.rem(z + k, zs)
+        piece = flipped[pl.ds(pl.multiple_of(to_z * strip, strip), strip), :]
+        terms[pl.ds(to_z * QUAD, QUAD)] = fold(dot_low(piece, weight)).reshape(QUAD, block, rank)
+        for t in range(QUAD):
+            if (k, t) != (0, 0):
+                peer = ahead(k, t)
+                term_copies[k, t] = copy(
+                    terms.at[peer], terms_in.at[k, t], term_s.at[k, t], term_r.at[k, t], peer, tm
+                )
     for made in fwd_copies:
         made.wait_recv()
     run_gram = self_gram(halves[...].reshape(n * m * half, rank))
     time_gram = self_gram(times_flat[...])
     own = bin_ref[pl.ds(pl.multiple_of(flat * block, block), block), :]
     scale = own / dot_f32(own, run_gram * time_gram)
-    three_copies = {}
-    for k in order:
-        one_copies[k, 0].wait_recv()
-        two_copies[k].wait_recv()
-        terms_last[k] = terms[place(z_of[k], 0, 0)] + terms_one[k, 0] + terms_two[k]
-        if k > 0:
-            three_copies[k] = copy(
-                terms_last.at[k], terms_three.at[k], three_s.at[k], three_r.at[k],
-                place(z_of[k], 0, 0), tm,
+    total = terms[me]
+    for k, t in steps:
+        term_copies[k, t].wait_recv()
+        total = total + terms_in[k, t]
+    bins_all[flat] = scale * total
+
+    bin_copies = {}
+    for k, t in steps:
+        bin_copies[k, t] = copy(
+            bins_all.at[flat], bins_all.at[flat], bin_s.at[k, t], bin_r.at[k, t], ahead(k, t), tm
+        )
+    other = lax.rem(tm + 1, m)
+    pass_copies = {}
+
+    def hand_on(k):
+        for t in range(QUAD):
+            if (k, t) != (0, 0):
+                bin_copies[k, t].wait_recv()
+            slot = tm * n + behind(k, t)
+            pass_copies[k, t] = copy(
+                bins_all.at[slot], bins_all.at[slot], pass_s.at[k, t], pass_r.at[k, t], me, other
             )
-    total = terms_last[0]
-    for k in range(1, zs):
-        three_copies[k].wait_recv()
-        total = total + terms_three[k]
-    bins_all[flat] = scale * total
-
-    z_copies = {}
-    for k in range(1, zs):
-        z_copies[k] = copy(
-            bins_all.at[flat], bins_all.at[flat], z_s.at[k], z_r.at[k],
-            place(z_of[k], 0, 0), tm,
-        )
-    from_z = [lax.rem(z - k + zs, zs) for k in range(zs)]
-    near_copies, far_copies, pass_copies = {}, {}, {}
-
-    def send_on(store, key, slot, sends, recvs, run_index, tm_index):
-        store[key] = copy(
-            bins_all.at[slot], bins_all.at[slot], sends.at[key], recvs.at[key],
-            run_index, tm_index,
-        )
-
-    other = lax.rem(tm + 1, m)
-    for k in range(zs):
-        if k > 0:
-            z_copies[k].wait_recv()
-        slot = tm * n + place(from_z[k], 0, 0)
-        send_on(near_copies, k, slot, near_s, near_r, partner_two, tm)
-        send_on(far_copies, (k, 0), slot, far_s, far_r, partner_one, tm)
-        send_on(pass_copies, (k, 0), slot, pass_s, pass_r, me, other)
-    for k in range(zs):
-        near_copies[k].wait_recv()
-        slot = tm * n + place(from_z[k], 0, 1)
-        send_on(far_copies, (k, 1), slot, far_s, far_r, partner_one, tm)
-        send_on(pass_copies, (k, 1), slot, pass_s, pass_r, me, other)
-    for k in range(zs):
-        for flip in (0, 1):
-            far_copies[k, flip].wait_recv()
-            slot = tm * n + place(from_z[k], 1, flip)
-            send_on(pass_copies, (k, 2 + flip), slot, pass_s, pass_r, me, other)
-    bin_gram = None
+
     writes = []
-    for k in range(zs):
-        for index in range(QUAD):
-            pass_copies[k, index].wait_recv()
+
+    def use(k, bin_gram):
+        from_z = lax.rem(z - k + zs, zs)
+        for t in range(QUAD):
+            pass_copies[k, t].wait_recv()
         pieces = []
         for core in range(m):
-            mine = pl.ds(core * n + from_z[k] * QUAD, QUAD)
+            mine = pl.ds(core * n + from_z * QUAD, QUAD)
             pieces.append(bins_all[mine].reshape(strip, rank))
-            made = pltpu.make_async_copy(
-                bins_all.at[mine], bin_out.at[mine], out_sem.at[k, core]
-            )
+            made = pltpu.make_async_copy(bins_all.at[mine], bin_out.at[mine], out_sem.at[k, core])
             made.start()
             writes.append(made)
         bins = jnp.concatenate(pieces, axis=0)
         bins_low = bins.astype(BF16)
         some = self_gram(bins)
-        bin_gram = some if k == 0 else bin_gram + some
         for off in range(m):
             slab = jnp.concatenate(
                 [
-                    slabs[off, :, pl.ds(pl.multiple_of(core * span + from_z[k] * strip, strip), strip)]
+                    slabs[off, :, pl.ds(pl.multiple_of(core * span + from_z * strip, strip), strip)]
                     for core in range(m)
                 ],
                 axis=1,
             )
             product = dot_low(slab, bins_low)
             inner_sum[off] = product if k == 0 else inner_sum[off] + product
+        return some if bin_gram is None else bin_gram + some
+
+    bin_gram = None
+    hand_on(0)
+    for k in range(1, zs):
+        hand_on(k)
+        bin_gram = use(k - 1, bin_gram)
+    bin_gram = use(zs - 1, bin_gram)
     run_terms = None
     for off in range(m):
         index = lax.rem(tm + off, m)
@@ -368,24 +335,27 @@
 
     for made in part_copies + wide_copies + half_copies + row_copies + fwd_copies:
         made.wait_send()
-    for store in (
-        one_copies, two_copies, three_copies, z_copies, near_copies, far_copies, pass_copies
-    ):
+    for store in (term_copies, bin_copies, pass_copies):
         for made in store.values():
             made.wait_send()
     for made in writes:
         made.wait()
 
 
-def hand_out(*refs):
-    count = (len(refs) - 1) // 2
-    sems = refs[-1]
-    copies = [
-        pltpu.make_async_copy(refs[i], refs[count + i], sems.at[i]) for i in range(count)
-    ]
-    for made in copies:
+def hand_out(run_in, bin_in, time_in, run_out, bin_out, time_out, runs, bins, times, in_s, out_s):
+    size = bins.shape[0] // QUAD
+    moves = [(run_in, runs, run_out), (time_in, times, time_out)]
+    for index in range(QUAD):
+        mine = pl.ds(index * size, size)
+        moves.append((bin_in.at[mine], bins.at[mine], bin_out.at[mine]))
+    loads = [pltpu.make_async_copy(a, b, in_s.at[i]) for i, (a, b, _) in enumerate(moves)]
+    stores = [pltpu.make_async_copy(b, c, out_s.at[i]) for i, (_, b, c) in enumerate(moves)]
+    for made in loads:
         made.start()
-    for made in copies:
+    for load, store in zip(loads, stores):
+        load.wait()
+        store.start()
+    for made in stores:
         made.wait()
 
 
@@ -418,11 +388,7 @@
             pltpu.VMEM((m, rows * kk, jj), F32),
             pltpu.VMEM((jj // m, m * rows * kk), BF16),
             pltpu.VMEM((n, block, rank), F32),
-            pltpu.VMEM((zs, 2, block, rank), F32),
-            pltpu.VMEM((zs, block, rank), F32),
-            pltpu.VMEM((zs, block, rank), F32),
-            pltpu.VMEM((zs, block, rank), F32),
-            pltpu.VMEM((zs, block, rank), F32),
+            pltpu.VMEM((zs, QUAD, block, rank), F32),
             pltpu.VMEM((n * m, block, rank), F32),
             pltpu.VMEM((m, rows * kk, rank), F32),
             pltpu.VMEM((n * m, half, rank), F32),
@@ -432,8 +398,7 @@
             pltpu.VMEM((n * m, rank), F32),
             dma((5,)), dma((m,)), dma((m,)), dma((n,)), dma((n,)), dma((m,)), dma((m,)),
             dma((n,)), dma((n,)), dma((n * m,)), dma((n * m,)),
-            dma((zs, 2)), dma((zs, 2)), dma((zs,)), dma((zs,)), dma((zs,)), dma((zs,)),
-            dma((zs,)), dma((zs,)), dma((zs,)), dma((zs,)), dma((zs, 2)), dma((zs, 2)),
+            dma((zs, QUAD)), dma((zs, QUAD)), dma((zs, QUAD)), dma((zs, QUAD)),
             dma((zs, QUAD)), dma((zs, QUAD)), dma((zs, m)),
         ],
         compiler_params=pltpu.CompilerParams(
@@ -445,7 +410,7 @@
         out_shape=shapes,
         in_specs=[anywhere] * 3,
         out_specs=[anywhere] * 3,
-        scratch_shapes=[dma((3,))],
+        scratch_shapes=[pltpu.VMEM(x.shape, F32) for x in shapes] + [dma((2 + QUAD,))] * 2,
         compiler_params=pltpu.CompilerParams(vmem_limit_bytes=VMEM_LIMIT),
     )(*results)
     return runs, bins.reshape(jj, rank), times

time: 59.3 us -> 38.6 us (0.65)
  the two profiles are of different devices: /device:TPU:1 before, /device:TPU:0 now
where the time goes in v3:
time: 38.6 us; the launch traced here: 38.4 us
  Pallas kernels  37.1 us (96%)
  between operations  1.28 us (3%)
    pallas_call x1, Pallas kernels, fused(): pl.pallas_call(functools.partial(kernel, n, m), out_shape=shapes, in_spec...  35.2 us
    pallas_call x1, Pallas kernels, fused(): pl.pallas_call(hand_out, out_shape=shapes, in_specs=[anywhere] * 3, out_s...  1.89 us

profile of v3, /device:TPU:0, one launch (start us, length us, event | category | flops | bytes accessed | tf_op | source)
XLA Modules:
  0.0 38.4 jit_solution(13299549769952365206)
XLA Ops:
  1.3 35.2 %shard_map.76 = (f32[16,128]{1,0:T(8,128)}, f32[32,32,128]{2,1,0:T(8,128)}, f32[16,128]{1,0:T(8,128)}) custom-call(s32[1]{0:T(128)S(6)} %copy.8.count_in, bf16[256,1024]{1,0:T(8,128)(2,1)} %bitcast.2, f32[16,128]{1,0:T(8,128)} %run_in.1, f32[1024,128]{1,0:T(8,128)} %bin_in.1, f32[16,128]{1,0:T(8,128)} %time_in.1), custom_call_target="tpu_custom_call" | custom-call | tf_op jit(solution)/shard_map/pallas_call | solution.py:376
  36.5 1.9 %shard_map.77 = (f32[16,128]{1,0:T(8,128)}, f32[32,32,128]{2,1,0:T(8,128)}, f32[16,128]{1,0:T(8,128)}) custom-call(f32[16,128]{1,0:T(8,128)} %get-tuple-element.9.run_in, f32[32,32,128]{2,1,0:T(8,128)} %get-tuple-element.10.bin_in, f32[16,128]{1,0:T(8,128)} %get-tuple-element.11.time_in), custom_call_target="tpu_custom_call" | custom-call | tf_op jit(solution)/shard_map/pallas_call | solution.py:408

commit v4 on v3

--- a/solution.py
+++ b/solution.py
@@ -118,7 +118,7 @@
     run_out, bin_out, time_out,
     count_ref, slabs, run_ref, bin_ref, time_ref,
     wide, wide_in, flipped, terms, terms_in,
-    bins_all, inner_sum, halves, parts, parts_in, times_all, times_flat,
+    bins_all, inner_sum, gram_sum, halves, parts, parts_in, times_all, times_flat,
     load_sem, wide_s, wide_r, half_s, half_r, fwd_s, fwd_r, part_s, part_r, row_s, row_r,
     term_s, term_r, bin_s, bin_r, pass_s, pass_r, out_sem,
 ):
@@ -133,24 +133,27 @@
     flat = tm * n + me
     zs = n // QUAD
     strip = QUAD * block
-
+    other = 1 - tm
     z = me // QUAD
     q = lax.rem(me, QUAD)
-    steps = [(k, t) for k in list(range(1, zs)) + [0] for t in range(QUAD) if (k, t) != (0, 0)]
-
-    def ahead(k, t):
-        return lax.rem(z + k, zs) * QUAD + lax.rem(q + t, QUAD)
-
-    def behind(k, t):
-        return lax.rem(z - k + zs, zs) * QUAD + lax.rem(q - t + QUAD, QUAD)
-
-    def copy(src, dst, send, recv, run_index, tm_index):
-        made = pltpu.make_async_remote_copy(
+
+    def ahead(index):
+        return lax.rem(z + index // QUAD, zs) * QUAD + lax.rem(q + index, QUAD)
+
+    def move(src, dst, send, recv, run_index, tm_index):
+        return pltpu.make_async_remote_copy(
             src_ref=src, dst_ref=dst, send_sem=send, recv_sem=recv,
             device_id=(run_index, tm_index), device_id_type=MESH,
         )
-        made.start()
-        return made
+
+    def all_of(ref, send, recv):
+        return move(ref, ref, send, recv, me, other)
+
+    def loop(low, high, body):
+        lax.fori_loop(low, high, lambda i, c: (body(i), c)[1], 0)
+
+    def aligned(value, unit):
+        return pl.ds(pl.multiple_of(value * unit, unit), unit)
 
     loads = [
         pltpu.make_async_copy(src, dst, load_sem.at[index])
@@ -163,183 +166,188 @@
         made.start()
 
     barrier = pltpu.get_barrier_semaphore()
-    for off in range(1, n * m):
+
+    def greet(off):
         peer = lax.rem(flat + off, n * m)
         pl.semaphore_signal(
             barrier, inc=1, device_id=(lax.rem(peer, n), peer // n), device_id_type=MESH
         )
+
+    loop(1, n * m, greet)
     for made in loads:
         made.wait()
 
     live = (lax.broadcasted_iota(jnp.int32, (rows, rank), 0) < count_ref[0]).astype(F32)
     runs = run_ref[...] * live
     halves[flat] = jnp.where(tm == 0, runs[:half], runs[rows - half:])
-    tensor = slabs[0]
-    times = time_ref[...]
-    inner = dot_low(tensor, bin_ref[...].astype(BF16)).reshape(rows, kk, rank)
+    inner = dot_low(slabs[0], bin_ref[...].astype(BF16)).reshape(rows, kk, rank)
     upper = inner[0] * runs[0:1]
     for i in range(1, rows):
         upper = upper + inner[i] * runs[i:i + 1]
-    lower = dot_f32(times, self_gram(runs) * self_gram(bin_ref[...]))
+    gram_sum[...] = jnp.zeros_like(gram_sum)
+
+    def gram_step(i):
+        gram_sum[...] += self_gram(bin_ref[aligned(i, jj // zs), :])
+
+    loop(0, zs, gram_step)
+    lower = dot_f32(time_ref[...], self_gram(runs) * gram_sum[...])
     both = jnp.concatenate([upper, lower], axis=1)
     for k in range(kk):
         parts[k] = both[k:k + 1]
 
     pl.semaphore_wait(barrier, n * m - 1)
 
-    part_copies = []
+    def send_part(off):
+        peer = lax.rem(me + off, n)
+        move(parts.at[peer], parts_in.at[off], part_s, part_r, peer, tm).start()
+
+    loop(1, n, send_part)
+
+    chunk = rows * kk // 8
+
+    def widen(i):
+        wide[aligned(i, chunk), :] = slabs[0, aligned(i, chunk), :].astype(F32)
+
+    loop(0, 8, widen)
+    wide_copy = move(wide, wide_in, wide_s, wide_r, me, other)
+    wide_copy.start()
+
+    def send_half(off):
+        peer = lax.rem(me + off, n)
+        move(halves.at[flat], halves.at[flat], half_s, half_r, peer, tm).start()
+
+    loop(1, n, send_half)
+
+    def flip(source, place):
+        def step(i):
+            columns = aligned(tm * (span // strip) + i, strip)
+            flipped[aligned(i, strip), place * rows * kk:(place + 1) * rows * kk] = (
+                source[:, columns].T.astype(BF16)
+            )
+
+        loop(0, span // strip, step)
+
+    flip(wide, 0)
+
+    others = pl.ds(1, n - 1)
+    all_of(parts_in.at[others], part_s, part_r).wait_recv()
+    total = parts[me]
     for off in range(1, n):
-        peer = lax.rem(me + off, n)
-        part_copies.append(
-            copy(parts.at[peer], parts_in.at[off], part_s.at[off], part_r.at[off], peer, tm)
-        )
-    wide[...] = tensor.astype(F32)
-    wide_copies = []
-    for off in range(1, m):
-        peer = lax.rem(tm + off, m)
-        wide_copies.append(
-            copy(wide, wide_in.at[off], wide_s.at[off], wide_r.at[off], me, peer)
-        )
-    half_copies = []
-    for off in range(1, n):
-        peer = lax.rem(me + off, n)
-        half_copies.append(
-            copy(halves.at[flat], halves.at[flat], half_s.at[off], half_r.at[off], peer, tm)
-        )
-
-    start = pl.multiple_of(tm * span, span)
-    flipped[:, : rows * kk] = wide[:, pl.ds(start, span)].T.astype(BF16)
-
-    total = parts[me]
-    for made, off in zip(part_copies, range(1, n)):
-        made.wait_recv()
         total = total + parts_in[off]
     times_all[flat] = time_ref[pl.ds(me, 1), :] * total[:, :rank] / total[:, rank:]
-    row_copies = []
-    for off in range(1, n * m):
+
+    def send_row(off):
         peer = lax.rem(flat + off, n * m)
-        row_copies.append(
-            copy(
-                times_all.at[flat], times_all.at[flat], row_s.at[off], row_r.at[off],
-                lax.rem(peer, n), peer // n,
-            )
-        )
-    for made in half_copies:
-        made.wait_recv()
-    fwd_copies = []
+        move(
+            times_all.at[flat], times_all.at[flat], row_s, row_r, lax.rem(peer, n), peer // n
+        ).start()
+
+    loop(1, n * m, send_row)
+    all_of(halves.at[others], half_s, half_r).wait_recv()
     mine = pl.ds(tm * n, n)
-    for off in range(1, m):
-        peer = lax.rem(tm + off, m)
-        fwd_copies.append(
-            copy(halves.at[mine], halves.at[mine], fwd_s.at[off], fwd_r.at[off], me, peer)
-        )
-    for off in range(1, m):
-        wide_copies[off - 1].wait_recv()
-        slabs[off] = wide_in[off].astype(BF16)
-        flipped[:, off * rows * kk:(off + 1) * rows * kk] = (
-            wide_in[off, :, pl.ds(start, span)].T.astype(BF16)
-        )
-    for made in row_copies:
-        made.wait_recv()
+    fwd_copy = move(halves.at[mine], halves.at[mine], fwd_s, fwd_r, me, other)
+    fwd_copy.start()
+    wide_copy.wait_recv()
+    flip(wide_in, 1)
+
+    def narrow(i):
+        slabs[1, aligned(i, chunk), :] = wide_in[aligned(i, chunk), :].astype(BF16)
+
+    loop(0, 8, narrow)
+    all_of(parts_in.at[others], part_s, part_r).wait_send()
+    all_of(halves.at[others], half_s, half_r).wait_send()
+    wide_copy.wait_send()
+    all_of(times_all.at[pl.ds(1, n * m - 1)], row_s, row_r).wait_recv()
     for k in range(n * m):
         times_flat[k:k + 1, :] = times_all[k]
 
     weights = []
-    for off in range(m):
-        index = lax.rem(tm + off, m)
-        low = times_flat[pl.ds(pl.multiple_of(index * kk, kk), kk), :].astype(BF16).astype(F32)
+    for index in (tm, other):
+        low = times_flat[aligned(index, kk), :].astype(BF16).astype(F32)
         weights.extend(low * runs[i:i + 1] for i in range(rows))
     weight = jnp.concatenate(split(jnp.concatenate(weights, axis=0)), axis=1)
-    term_copies = {}
+
+    def send_term(index):
+        peer = ahead(index)
+        move(terms.at[peer], terms_in.at[index], term_s, term_r, peer, tm).start()
+
     for k in list(range(1, zs)) + [0]:
         to_z = lax.rem(z + k, zs)
-        piece = flipped[pl.ds(pl.multiple_of(to_z * strip, strip), strip), :]
+        piece = flipped[aligned(to_z, strip), :]
         terms[pl.ds(to_z * QUAD, QUAD)] = fold(dot_low(piece, weight)).reshape(QUAD, block, rank)
-        for t in range(QUAD):
-            if (k, t) != (0, 0):
-                peer = ahead(k, t)
-                term_copies[k, t] = copy(
-                    terms.at[peer], terms_in.at[k, t], term_s.at[k, t], term_r.at[k, t], peer, tm
-                )
-    for made in fwd_copies:
-        made.wait_recv()
+        loop(max(k * QUAD, 1), (k + 1) * QUAD, send_term)
+    all_of(times_all.at[pl.ds(1, n * m - 1)], row_s, row_r).wait_send()
+    fwd_copy.wait()
     run_gram = self_gram(halves[...].reshape(n * m * half, rank))
     time_gram = self_gram(times_flat[...])
-    own = bin_ref[pl.ds(pl.multiple_of(flat * block, block), block), :]
+    own = bin_ref[aligned(flat, block), :]
     scale = own / dot_f32(own, run_gram * time_gram)
+    gram_sum[...] = jnp.zeros_like(gram_sum)
+    inner_sum[...] = jnp.zeros_like(inner_sum)
     total = terms[me]
-    for k, t in steps:
-        term_copies[k, t].wait_recv()
-        total = total + terms_in[k, t]
+    all_of(terms_in.at[others], term_s, term_r).wait_recv()
+    for index in range(1, n):
+        total = total + terms_in[index]
     bins_all[flat] = scale * total
 
-    bin_copies = {}
-    for k, t in steps:
-        bin_copies[k, t] = copy(
-            bins_all.at[flat], bins_all.at[flat], bin_s.at[k, t], bin_r.at[k, t], ahead(k, t), tm
-        )
-    other = lax.rem(tm + 1, m)
-    pass_copies = {}
+    def send_bins(index):
+        move(
+            bins_all.at[flat], bins_all.at[flat], bin_s, bin_r.at[index // QUAD], ahead(index), tm
+        ).start()
+
+    loop(1, n, send_bins)
+    all_of(terms_in.at[others], term_s, term_r).wait_send()
+
+    def group(core, k):
+        return pl.ds(core * n + lax.rem(z - k + zs, zs) * QUAD, QUAD)
 
     def hand_on(k):
-        for t in range(QUAD):
-            if (k, t) != (0, 0):
-                bin_copies[k, t].wait_recv()
-            slot = tm * n + behind(k, t)
-            pass_copies[k, t] = copy(
-                bins_all.at[slot], bins_all.at[slot], pass_s.at[k, t], pass_r.at[k, t], me, other
-            )
-
-    writes = []
-
-    def use(k, bin_gram):
+        mine = bins_all.at[group(tm, k)]
+        move(mine, mine, pass_s, pass_r.at[k], me, other).start()
+
+    all_of(bins_all.at[pl.ds(0, QUAD - 1)], bin_s, bin_r.at[0]).wait_recv()
+    hand_on(0)
+
+    def arrive(k):
+        all_of(bins_all.at[group(tm, k)], bin_s, bin_r.at[k]).wait_recv()
+        hand_on(k)
+
+    loop(1, zs, arrive)
+
+    def use(k):
         from_z = lax.rem(z - k + zs, zs)
-        for t in range(QUAD):
-            pass_copies[k, t].wait_recv()
+        all_of(bins_all.at[group(other, k)], pass_s, pass_r.at[k]).wait_recv()
         pieces = []
         for core in range(m):
-            mine = pl.ds(core * n + from_z * QUAD, QUAD)
+            mine = group(core, k)
             pieces.append(bins_all[mine].reshape(strip, rank))
-            made = pltpu.make_async_copy(bins_all.at[mine], bin_out.at[mine], out_sem.at[k, core])
-            made.start()
-            writes.append(made)
+            pltpu.make_async_copy(bins_all.at[mine], bin_out.at[mine], out_sem.at[k, core]).start()
         bins = jnp.concatenate(pieces, axis=0)
         bins_low = bins.astype(BF16)
-        some = self_gram(bins)
+        gram_sum[...] += self_gram(bins)
         for off in range(m):
             slab = jnp.concatenate(
-                [
-                    slabs[off, :, pl.ds(pl.multiple_of(core * span + from_z * strip, strip), strip)]
-                    for core in range(m)
-                ],
-                axis=1,
+                [slabs[off, :, aligned(core * zs + from_z, strip)] for core in range(m)], axis=1
             )
-            product = dot_low(slab, bins_low)
-            inner_sum[off] = product if k == 0 else inner_sum[off] + product
-        return some if bin_gram is None else bin_gram + some
-
-    bin_gram = None
-    hand_on(0)
-    for k in range(1, zs):
-        hand_on(k)
-        bin_gram = use(k - 1, bin_gram)
-    bin_gram = use(zs - 1, bin_gram)
+            inner_sum[off] += dot_low(slab, bins_low)
+
+    loop(0, zs, use)
     run_terms = None
-    for off in range(m):
-        index = lax.rem(tm + off, m)
-        weight = times_flat[pl.ds(pl.multiple_of(index * kk, kk), kk), :]
+    for off, index in enumerate((tm, other)):
+        weight = times_flat[aligned(index, kk), :]
         some = jnp.sum(inner_sum[off].reshape(rows, kk, rank) * weight[None], axis=1)
         run_terms = some if run_terms is None else run_terms + some
-    run_out[...] = runs * run_terms / (dot_f32(runs, bin_gram * time_gram) + 1.0 - live)
-    time_out[...] = times_flat[pl.ds(pl.multiple_of(tm * kk, kk), kk), :]
-
-    for made in part_copies + wide_copies + half_copies + row_copies + fwd_copies:
-        made.wait_send()
-    for store in (term_copies, bin_copies, pass_copies):
-        for made in store.values():
-            made.wait_send()
-    for made in writes:
-        made.wait()
+    run_out[...] = runs * run_terms / (dot_f32(runs, gram_sum[...] * time_gram) + 1.0 - live)
+    time_out[...] = times_flat[aligned(tm, kk), :]
+    all_of(bins_all.at[others], bin_s, bin_r.at[0]).wait_send()
+    all_of(bins_all.at[mine], pass_s, pass_r.at[0]).wait_send()
+
+    def finish(k):
+        for core in range(m):
+            mine = group(core, k)
+            pltpu.make_async_copy(bins_all.at[mine], bin_out.at[mine], out_sem.at[k, core]).wait()
+
+    loop(0, zs, finish)
 
 
 def hand_out(run_in, bin_in, time_in, run_out, bin_out, time_out, runs, bins, times, in_s, out_s):
@@ -385,21 +393,19 @@
             pltpu.VMEM((jj, rank), F32),
             pltpu.VMEM((kk, rank), F32),
             pltpu.VMEM((rows * kk, jj), F32),
-            pltpu.VMEM((m, rows * kk, jj), F32),
+            pltpu.VMEM((rows * kk, jj), F32),
             pltpu.VMEM((jj // m, m * rows * kk), BF16),
             pltpu.VMEM((n, block, rank), F32),
-            pltpu.VMEM((zs, QUAD, block, rank), F32),
+            pltpu.VMEM((n, block, rank), F32),
             pltpu.VMEM((n * m, block, rank), F32),
             pltpu.VMEM((m, rows * kk, rank), F32),
+            pltpu.VMEM((rank, rank), F32),
             pltpu.VMEM((n * m, half, rank), F32),
             pltpu.VMEM((n, 1, 2 * rank), F32),
             pltpu.VMEM((n, 1, 2 * rank), F32),
             pltpu.VMEM((n * m, 1, rank), F32),
             pltpu.VMEM((n * m, rank), F32),
-            dma((5,)), dma((m,)), dma((m,)), dma((n,)), dma((n,)), dma((m,)), dma((m,)),
-            dma((n,)), dma((n,)), dma((n * m,)), dma((n * m,)),
-            dma((zs, QUAD)), dma((zs, QUAD)), dma((zs, QUAD)), dma((zs, QUAD)),
-            dma((zs, QUAD)), dma((zs, QUAD)), dma((zs, m)),
+            dma((5,)), *[dma] * 12, dma, dma((zs,)), dma, dma((zs,)), dma((zs, m)),
         ],
         compiler_params=pltpu.CompilerParams(
             collective_id=0, has_side_effects=True, vmem_limit_bytes=VMEM_LIMIT

time: 38.6 us -> 36 us (0.933)
  the two profiles are of different devices: /device:TPU:0 before, /device:TPU:1 now
where the time goes in v4:
time: 36 us; the launch traced here: 35.8 us
  Pallas kernels  34.5 us (96%)
  between operations  1.28 us (4%)
    pallas_call x1, Pallas kernels, fused(): pl.pallas_call(functools.partial(kernel, n, m), out_shape=shapes, in_spec...  32.6 us
    pallas_call x1, Pallas kernels, fused(): pl.pallas_call(hand_out, out_shape=shapes, in_specs=[anywhere] * 3, out_s...  1.89 us

profile of v4, /device:TPU:1, one launch (start us, length us, event | category | flops | bytes accessed | tf_op | source)
XLA Modules:
  0.0 35.8 jit_solution(1560219083840819263)
XLA Ops:
  1.3 32.6 %shard_map.76 = (f32[16,128]{1,0:T(8,128)}, f32[32,32,128]{2,1,0:T(8,128)}, f32[16,128]{1,0:T(8,128)}) custom-call(s32[1]{0:T(128)S(6)} %copy.8.count_in, bf16[256,1024]{1,0:T(8,128)(2,1)} %bitcast.2, f32[16,128]{1,0:T(8,128)} %run_in.1, f32[1024,128]{1,0:T(8,128)} %bin_in.1, f32[16,128]{1,0:T(8,128)} %time_in.1), custom_call_target="tpu_custom_call" | custom-call | tf_op jit(solution)/shard_map/pallas_call | solution.py:384
  33.9 1.9 %shard_map.77 = (f32[16,128]{1,0:T(8,128)}, f32[32,32,128]{2,1,0:T(8,128)}, f32[16,128]{1,0:T(8,128)}) custom-call(f32[16,128]{1,0:T(8,128)} %get-tuple-element.9.run_in, f32[32,32,128]{2,1,0:T(8,128)} %get-tuple-element.10.bin_in, f32[16,128]{1,0:T(8,128)} %get-tuple-element.11.time_in), custom_call_target="tpu_custom_call" | custom-call | tf_op jit(solution)/shard_map/pallas_call | solution.py:414

commit v5 on v4

--- a/solution.py
+++ b/solution.py
@@ -120,7 +120,7 @@
     wide, wide_in, flipped, terms, terms_in,
     bins_all, inner_sum, gram_sum, halves, parts, parts_in, times_all, times_flat,
     load_sem, wide_s, wide_r, half_s, half_r, fwd_s, fwd_r, part_s, part_r, row_s, row_r,
-    term_s, term_r, bin_s, bin_r, pass_s, pass_r, out_sem,
+    term_s, term_r, bin_s, bin_r, along_r, pass_s, pass_r, out_sem,
 ):
     me = lax.axis_index("runs")
     tm = lax.axis_index("tm")
@@ -290,29 +290,37 @@
         total = total + terms_in[index]
     bins_all[flat] = scale * total
 
-    def send_bins(index):
-        move(
-            bins_all.at[flat], bins_all.at[flat], bin_s, bin_r.at[index // QUAD], ahead(index), tm
-        ).start()
-
-    loop(1, n, send_bins)
-    all_of(terms_in.at[others], term_s, term_r).wait_send()
-
     def group(core, k):
         return pl.ds(core * n + lax.rem(z - k + zs, zs) * QUAD, QUAD)
 
+    def send_along(k):
+        mine = bins_all.at[flat]
+        move(mine, mine, bin_s, along_r.at[k], ahead(k * QUAD), tm).start()
+
+    def send_around(k):
+        held = bins_all.at[tm * n + lax.rem(z - k + zs, zs) * QUAD + q]
+
+        def step(t):
+            move(held, held, bin_s, bin_r.at[k], ahead(t), tm).start()
+
+        loop(1, QUAD, step)
+
+    loop(1, zs, send_along)
+    send_around(0)
+    all_of(terms_in.at[others], term_s, term_r).wait_send()
+
+    def relay(k):
+        all_of(bins_all.at[0], bin_s, along_r.at[k]).wait_recv()
+        send_around(k)
+
+    loop(1, zs, relay)
+
     def hand_on(k):
+        all_of(bins_all.at[pl.ds(0, QUAD - 1)], bin_s, bin_r.at[k]).wait_recv()
         mine = bins_all.at[group(tm, k)]
         move(mine, mine, pass_s, pass_r.at[k], me, other).start()
 
-    all_of(bins_all.at[pl.ds(0, QUAD - 1)], bin_s, bin_r.at[0]).wait_recv()
-    hand_on(0)
-
-    def arrive(k):
-        all_of(bins_all.at[group(tm, k)], bin_s, bin_r.at[k]).wait_recv()
-        hand_on(k)
-
-    loop(1, zs, arrive)
+    loop(0, zs, hand_on)
 
     def use(k):
         from_z = lax.rem(z - k + zs, zs)
@@ -405,7 +413,7 @@
             pltpu.VMEM((n, 1, 2 * rank), F32),
             pltpu.VMEM((n * m, 1, rank), F32),
             pltpu.VMEM((n * m, rank), F32),
-            dma((5,)), *[dma] * 12, dma, dma((zs,)), dma, dma((zs,)), dma((zs, m)),
+            dma((5,)), *[dma] * 12, dma, dma((zs,)), dma((zs,)), dma, dma((zs,)), dma((zs, m)),
         ],
         compiler_params=pltpu.CompilerParams(
             collective_id=0, has_side_effects=True, vmem_limit_bytes=VMEM_LIMIT

time: 36 us -> 38.1 us (1.058)
  Pallas kernels: 34.5 us -> 36.6 us
    pallas_call x1, Pallas kernels: 32.6 us -> 34.7 us  [fused(): pl.pallas_call(functools.partial(kernel, n, m), out_shape=shapes, in_spec...]
where the time goes in v5:
time: 38.1 us; the launch traced here: 37.9 us
  Pallas kernels  36.6 us (96%)
  between operations  1.28 us (3%)
    pallas_call x1, Pallas kernels, fused(): pl.pallas_call(functools.partial(kernel, n, m), out_shape=shapes, in_spec...  34.7 us
    pallas_call x1, Pallas kernels, fused(): pl.pallas_call(hand_out, out_shape=shapes, in_specs=[anywhere] * 3, out_s...  1.89 us

profile of v5, /device:TPU:1, one launch (start us, length us, event | category | flops | bytes accessed | tf_op | source)
XLA Modules:
  0.0 37.9 jit_solution(7558551793907308871)
XLA Ops:
  1.3 34.7 %shard_map.76 = (f32[16,128]{1,0:T(8,128)}, f32[32,32,128]{2,1,0:T(8,128)}, f32[16,128]{1,0:T(8,128)}) custom-call(s32[1]{0:T(128)S(6)} %copy.8.count_in, bf16[256,1024]{1,0:T(8,128)(2,1)} %bitcast.2, f32[16,128]{1,0:T(8,128)} %run_in.1, f32[1024,128]{1,0:T(8,128)} %bin_in.1, f32[16,128]{1,0:T(8,128)} %time_in.1), custom_call_target="tpu_custom_call" | custom-call | tf_op jit(solution)/shard_map/pallas_call | solution.py:392
  36.0 1.9 %shard_map.77 = (f32[16,128]{1,0:T(8,128)}, f32[32,32,128]{2,1,0:T(8,128)}, f32[16,128]{1,0:T(8,128)}) custom-call(f32[16,128]{1,0:T(8,128)} %get-tuple-element.9.run_in, f32[32,32,128]{2,1,0:T(8,128)} %get-tuple-element.10.bin_in, f32[16,128]{1,0:T(8,128)} %get-tuple-element.11.time_in), custom_call_target="tpu_custom_call" | custom-call | tf_op jit(solution)/shard_map/pallas_call | solution.py:422

commit v6 on v4

--- a/solution.py
+++ b/solution.py
@@ -118,8 +118,8 @@
     run_out, bin_out, time_out,
     count_ref, slabs, run_ref, bin_ref, time_ref,
     wide, wide_in, flipped, terms, terms_in,
-    bins_all, inner_sum, gram_sum, halves, parts, parts_in, times_all, times_flat,
-    load_sem, wide_s, wide_r, half_s, half_r, fwd_s, fwd_r, part_s, part_r, row_s, row_r,
+    bins_all, inner_sum, runs_all, parts, parts_in, times_all, times_flat,
+    load_sem, wide_s, wide_r, half_s, half_r, part_s, part_r, row_s, row_r,
     term_s, term_r, bin_s, bin_r, pass_s, pass_r, out_sem,
 ):
     me = lax.axis_index("runs")
@@ -128,7 +128,6 @@
     kk = time_ref.shape[0]
     jj, rank = bin_ref.shape
     block = jj // (n * m)
-    half = rows // m
     span = jj // m
     flat = tm * n + me
     zs = n // QUAD
@@ -179,26 +178,19 @@
 
     live = (lax.broadcasted_iota(jnp.int32, (rows, rank), 0) < count_ref[0]).astype(F32)
     runs = run_ref[...] * live
-    halves[flat] = jnp.where(tm == 0, runs[:half], runs[rows - half:])
+    runs_all[me] = runs
     inner = dot_low(slabs[0], bin_ref[...].astype(BF16)).reshape(rows, kk, rank)
     upper = inner[0] * runs[0:1]
     for i in range(1, rows):
         upper = upper + inner[i] * runs[i:i + 1]
-    gram_sum[...] = jnp.zeros_like(gram_sum)
-
-    def gram_step(i):
-        gram_sum[...] += self_gram(bin_ref[aligned(i, jj // zs), :])
-
-    loop(0, zs, gram_step)
-    lower = dot_f32(time_ref[...], self_gram(runs) * gram_sum[...])
-    both = jnp.concatenate([upper, lower], axis=1)
     for k in range(kk):
-        parts[k] = both[k:k + 1]
+        parts[k] = upper[k:k + 1]
 
     pl.semaphore_wait(barrier, n * m - 1)
 
     def send_part(off):
         peer = lax.rem(me + off, n)
+        move(runs_all.at[me], runs_all.at[me], half_s, half_r, peer, tm).start()
         move(parts.at[peer], parts_in.at[off], part_s, part_r, peer, tm).start()
 
     loop(1, n, send_part)
@@ -212,11 +204,7 @@
     wide_copy = move(wide, wide_in, wide_s, wide_r, me, other)
     wide_copy.start()
 
-    def send_half(off):
-        peer = lax.rem(me + off, n)
-        move(halves.at[flat], halves.at[flat], half_s, half_r, peer, tm).start()
-
-    loop(1, n, send_half)
+    bin_gram = self_gram(bin_ref[...])
 
     def flip(source, place):
         def step(i):
@@ -227,14 +215,17 @@
 
         loop(0, span // strip, step)
 
-    flip(wide, 0)
-
     others = pl.ds(1, n - 1)
+    all_of(runs_all.at[others], half_s, half_r).wait_recv()
+    run_gram = self_gram(runs_all[...].reshape(n * rows, rank))
+    lower = dot_f32(time_ref[...], run_gram * bin_gram)
+    times_flat[pl.ds(0, kk), :] = time_ref[...] / lower
+    ratio = times_flat[pl.ds(me, 1), :]
     all_of(parts_in.at[others], part_s, part_r).wait_recv()
     total = parts[me]
     for off in range(1, n):
         total = total + parts_in[off]
-    times_all[flat] = time_ref[pl.ds(me, 1), :] * total[:, :rank] / total[:, rank:]
+    times_all[flat] = ratio * total
 
     def send_row(off):
         peer = lax.rem(flat + off, n * m)
@@ -243,19 +234,12 @@
         ).start()
 
     loop(1, n * m, send_row)
-    all_of(halves.at[others], half_s, half_r).wait_recv()
-    mine = pl.ds(tm * n, n)
-    fwd_copy = move(halves.at[mine], halves.at[mine], fwd_s, fwd_r, me, other)
-    fwd_copy.start()
+    flip(wide, 0)
     wide_copy.wait_recv()
     flip(wide_in, 1)
 
-    def narrow(i):
-        slabs[1, aligned(i, chunk), :] = wide_in[aligned(i, chunk), :].astype(BF16)
-
-    loop(0, 8, narrow)
     all_of(parts_in.at[others], part_s, part_r).wait_send()
-    all_of(halves.at[others], half_s, half_r).wait_send()
+    all_of(runs_all.at[others], half_s, half_r).wait_send()
     wide_copy.wait_send()
     all_of(times_all.at[pl.ds(1, n * m - 1)], row_s, row_r).wait_recv()
     for k in range(n * m):
@@ -277,13 +261,14 @@
         terms[pl.ds(to_z * QUAD, QUAD)] = fold(dot_low(piece, weight)).reshape(QUAD, block, rank)
         loop(max(k * QUAD, 1), (k + 1) * QUAD, send_term)
     all_of(times_all.at[pl.ds(1, n * m - 1)], row_s, row_r).wait_send()
-    fwd_copy.wait()
-    run_gram = self_gram(halves[...].reshape(n * m * half, rank))
     time_gram = self_gram(times_flat[...])
     own = bin_ref[aligned(flat, block), :]
     scale = own / dot_f32(own, run_gram * time_gram)
-    gram_sum[...] = jnp.zeros_like(gram_sum)
-    inner_sum[...] = jnp.zeros_like(inner_sum)
+
+    def narrow(i):
+        slabs[1, aligned(i, chunk), :] = wide_in[aligned(i, chunk), :].astype(BF16)
+
+    loop(0, 8, narrow)
     total = terms[me]
     all_of(terms_in.at[others], term_s, term_r).wait_recv()
     for index in range(1, n):
@@ -303,7 +288,7 @@
 
     def hand_on(k):
         mine = bins_all.at[group(tm, k)]
-        move(mine, mine, pass_s, pass_r.at[k], me, other).start()
+        move(mine, mine, pass_s, pass_r, me, other).start()
 
     all_of(bins_all.at[pl.ds(0, QUAD - 1)], bin_s, bin_r.at[0]).wait_recv()
     hand_on(0)
@@ -314,40 +299,33 @@
 
     loop(1, zs, arrive)
 
-    def use(k):
-        from_z = lax.rem(z - k + zs, zs)
-        all_of(bins_all.at[group(other, k)], pass_s, pass_r.at[k]).wait_recv()
-        pieces = []
-        for core in range(m):
-            mine = group(core, k)
-            pieces.append(bins_all[mine].reshape(strip, rank))
-            pltpu.make_async_copy(bins_all.at[mine], bin_out.at[mine], out_sem.at[k, core]).start()
-        bins = jnp.concatenate(pieces, axis=0)
+    def use(core, index):
+        blocks = pl.ds(core * n, n)
+        write = pltpu.make_async_copy(bins_all.at[blocks], bin_out.at[blocks], out_sem.at[index])
+        write.start()
+        bins = bins_all[blocks].reshape(span, rank)
         bins_low = bins.astype(BF16)
-        gram_sum[...] += self_gram(bins)
-        for off in range(m):
-            slab = jnp.concatenate(
-                [slabs[off, :, aligned(core * zs + from_z, strip)] for core in range(m)], axis=1
-            )
-            inner_sum[off] += dot_low(slab, bins_low)
-
-    loop(0, zs, use)
+        sums = [dot_low(slabs[off, :, aligned(core, span)], bins_low) for off in range(m)]
+        return write, sums, self_gram(bins)
+
+    write_own, own_sums, own_gram = use(tm, 0)
+    for off in range(m):
+        inner_sum[off] = own_sums[off]
+    all_of(bins_all.at[pl.ds(other * n, n)], pass_s, pass_r).wait_recv()
+    write_other, other_sums, other_gram = use(other, 1)
+    mixing = (own_gram + other_gram) * time_gram
     run_terms = None
     for off, index in enumerate((tm, other)):
         weight = times_flat[aligned(index, kk), :]
-        some = jnp.sum(inner_sum[off].reshape(rows, kk, rank) * weight[None], axis=1)
+        whole = (inner_sum[off] + other_sums[off]).reshape(rows, kk, rank)
+        some = jnp.sum(whole * weight[None], axis=1)
         run_terms = some if run_terms is None else run_terms + some
-    run_out[...] = runs * run_terms / (dot_f32(runs, gram_sum[...] * time_gram) + 1.0 - live)
+    run_out[...] = runs * run_terms / (dot_f32(runs, mixing) + 1.0 - live)
     time_out[...] = times_flat[aligned(tm, kk), :]
     all_of(bins_all.at[others], bin_s, bin_r.at[0]).wait_send()
-    all_of(bins_all.at[mine], pass_s, pass_r.at[0]).wait_send()
-
-    def finish(k):
-        for core in range(m):
-            mine = group(core, k)
-            pltpu.make_async_copy(bins_all.at[mine], bin_out.at[mine], out_sem.at[k, core]).wait()
-
-    loop(0, zs, finish)
+    all_of(bins_all.at[pl.ds(0, n)], pass_s, pass_r).wait_send()
+    write_own.wait()
+    write_other.wait()
 
 
 def hand_out(run_in, bin_in, time_in, run_out, bin_out, time_out, runs, bins, times, in_s, out_s):
@@ -371,7 +349,6 @@
     rows, kk, jj = tensor.shape
     rank = bin_init.shape[1]
     block = jj // (n * m)
-    half = rows // m
     zs = n // QUAD
     dma = pltpu.SemaphoreType.DMA
     vmem = pl.BlockSpec(memory_space=pltpu.VMEM)
@@ -399,13 +376,12 @@
             pltpu.VMEM((n, block, rank), F32),
             pltpu.VMEM((n * m, block, rank), F32),
             pltpu.VMEM((m, rows * kk, rank), F32),
-            pltpu.VMEM((rank, rank), F32),
-            pltpu.VMEM((n * m, half, rank), F32),
-            pltpu.VMEM((n, 1, 2 * rank), F32),
-            pltpu.VMEM((n, 1, 2 * rank), F32),
+            pltpu.VMEM((n, rows, rank), F32),
+            pltpu.VMEM((n, 1, rank), F32),
+            pltpu.VMEM((n, 1, rank), F32),
             pltpu.VMEM((n * m, 1, rank), F32),
             pltpu.VMEM((n * m, rank), F32),
-            dma((5,)), *[dma] * 12, dma, dma((zs,)), dma, dma((zs,)), dma((zs, m)),
+            dma((5,)), *[dma] * 10, dma, dma((zs,)), dma, dma, dma((m,)),
         ],
         compiler_params=pltpu.CompilerParams(
             collective_id=0, has_side_effects=True, vmem_limit_bytes=VMEM_LIMIT
@@ -424,7 +400,7 @@
 
 def update(n, m, *args):
     rows, kk, jj = args[0].shape
-    fits = m == 2 and kk == n and n % QUAD == 0 and kk % 16 == 0 and rows % (8 * m) == 0
+    fits = m == 2 and kk == n and n % QUAD == 0 and kk % 16 == 0 and rows % 8 == 0
     fits = fits and jj % (8 * n * m) == 0 and (QUAD * jj // (n * m)) % 128 == 0
     return fused(n, m, *args) if fits else shards(*args)
 

time: 36 us -> 37.1 us (1.031)
  Pallas kernels: 34.5 us -> 35.6 us
    pallas_call x1, Pallas kernels: 32.6 us -> 33.7 us  [fused(): pl.pallas_call(functools.partial(kernel, n, m), out_shape=shapes, in_spec...]
where the time goes in v6:
time: 37.1 us; the launch traced here: 36.9 us
  Pallas kernels  35.6 us (96%)
  between operations  1.28 us (3%)
    pallas_call x1, Pallas kernels, fused(): pl.pallas_call(functools.partial(kernel, n, m), out_shape=shapes, in_spec...  33.7 us
    pallas_call x1, Pallas kernels, fused(): pl.pallas_call(hand_out, out_shape=shapes, in_specs=[anywhere] * 3, out_s...  1.89 us

profile of v6, /device:TPU:1, one launch (start us, length us, event | category | flops | bytes accessed | tf_op | source)
XLA Modules:
  0.0 36.9 jit_solution(13188563288064515621)
XLA Ops:
  1.3 33.7 %shard_map.76 = (f32[16,128]{1,0:T(8,128)}, f32[32,32,128]{2,1,0:T(8,128)}, f32[16,128]{1,0:T(8,128)}) custom-call(s32[1]{0:T(128)S(6)} %copy.8.count_in, bf16[256,1024]{1,0:T(8,128)(2,1)} %bitcast.2, f32[16,128]{1,0:T(8,128)} %run_in.1, f32[1024,128]{1,0:T(8,128)} %bin_in.1, f32[16,128]{1,0:T(8,128)} %time_in.1), custom_call_target="tpu_custom_call" | custom-call | tf_op jit(solution)/shard_map/pallas_call | solution.py:361
  35.0 1.9 %shard_map.77 = (f32[16,128]{1,0:T(8,128)}, f32[32,32,128]{2,1,0:T(8,128)}, f32[16,128]{1,0:T(8,128)}) custom-call(f32[16,128]{1,0:T(8,128)} %get-tuple-element.9.run_in, f32[32,32,128]{2,1,0:T(8,128)} %get-tuple-element.10.bin_in, f32[16,128]{1,0:T(8,128)} %get-tuple-element.11.time_in), custom_call_target="tpu_custom_call" | custom-call | tf_op jit(solution)/shard_map/pallas_call | solution.py:390

commit v7 on v4

--- a/solution.py
+++ b/solution.py
@@ -118,8 +118,8 @@
     run_out, bin_out, time_out,
     count_ref, slabs, run_ref, bin_ref, time_ref,
     wide, wide_in, flipped, terms, terms_in,
-    bins_all, inner_sum, gram_sum, halves, parts, parts_in, times_all, times_flat,
-    load_sem, wide_s, wide_r, half_s, half_r, fwd_s, fwd_r, part_s, part_r, row_s, row_r,
+    bins_all, inner_sum, gram_sum, runs_all, parts, parts_in, times_all, times_flat,
+    load_sem, wide_s, wide_r, half_s, half_r, part_s, part_r, row_s, row_r,
     term_s, term_r, bin_s, bin_r, pass_s, pass_r, out_sem,
 ):
     me = lax.axis_index("runs")
@@ -128,7 +128,6 @@
     kk = time_ref.shape[0]
     jj, rank = bin_ref.shape
     block = jj // (n * m)
-    half = rows // m
     span = jj // m
     flat = tm * n + me
     zs = n // QUAD
@@ -179,62 +178,61 @@
 
     live = (lax.broadcasted_iota(jnp.int32, (rows, rank), 0) < count_ref[0]).astype(F32)
     runs = run_ref[...] * live
-    halves[flat] = jnp.where(tm == 0, runs[:half], runs[rows - half:])
+    runs_all[me] = runs
     inner = dot_low(slabs[0], bin_ref[...].astype(BF16)).reshape(rows, kk, rank)
     upper = inner[0] * runs[0:1]
     for i in range(1, rows):
         upper = upper + inner[i] * runs[i:i + 1]
-    gram_sum[...] = jnp.zeros_like(gram_sum)
-
-    def gram_step(i):
-        gram_sum[...] += self_gram(bin_ref[aligned(i, jj // zs), :])
-
-    loop(0, zs, gram_step)
-    lower = dot_f32(time_ref[...], self_gram(runs) * gram_sum[...])
-    both = jnp.concatenate([upper, lower], axis=1)
     for k in range(kk):
-        parts[k] = both[k:k + 1]
+        parts[k] = upper[k:k + 1]
 
     pl.semaphore_wait(barrier, n * m - 1)
 
     def send_part(off):
         peer = lax.rem(me + off, n)
+        move(runs_all.at[me], runs_all.at[me], half_s, half_r, peer, tm).start()
         move(parts.at[peer], parts_in.at[off], part_s, part_r, peer, tm).start()
 
     loop(1, n, send_part)
 
     chunk = rows * kk // 8
 
-    def widen(i):
-        wide[aligned(i, chunk), :] = slabs[0, aligned(i, chunk), :].astype(F32)
-
-    loop(0, 8, widen)
-    wide_copy = move(wide, wide_in, wide_s, wide_r, me, other)
+    def widen(core):
+        def step(i):
+            wide[core, aligned(i, chunk), :] = slabs[
+                0, aligned(i, chunk), aligned(core, span)
+            ].astype(F32)
+
+        loop(0, 8, step)
+
+    widen(other)
+    wide_copy = move(wide.at[other], wide_in.at[other], wide_s.at[0], wide_r.at[0], me, other)
     wide_copy.start()
-
-    def send_half(off):
-        peer = lax.rem(me + off, n)
-        move(halves.at[flat], halves.at[flat], half_s, half_r, peer, tm).start()
-
-    loop(1, n, send_half)
+    widen(tm)
+    rest_copy = move(wide.at[tm], wide_in.at[tm], wide_s.at[1], wide_r.at[1], me, other)
+
+    bin_gram = self_gram(bin_ref[...])
 
     def flip(source, place):
         def step(i):
-            columns = aligned(tm * (span // strip) + i, strip)
             flipped[aligned(i, strip), place * rows * kk:(place + 1) * rows * kk] = (
-                source[:, columns].T.astype(BF16)
+                source[tm, :, aligned(i, strip)].T.astype(BF16)
             )
 
         loop(0, span // strip, step)
 
     flip(wide, 0)
-
     others = pl.ds(1, n - 1)
+    all_of(runs_all.at[others], half_s, half_r).wait_recv()
+    run_gram = self_gram(runs_all[...].reshape(n * rows, rank))
+    lower = dot_f32(time_ref[...], run_gram * bin_gram)
+    times_flat[pl.ds(0, kk), :] = time_ref[...] / lower
+    ratio = times_flat[pl.ds(me, 1), :]
     all_of(parts_in.at[others], part_s, part_r).wait_recv()
     total = parts[me]
     for off in range(1, n):
         total = total + parts_in[off]
-    times_all[flat] = time_ref[pl.ds(me, 1), :] * total[:, :rank] / total[:, rank:]
+    times_all[flat] = ratio * total
 
     def send_row(off):
         peer = lax.rem(flat + off, n * m)
@@ -243,19 +241,11 @@
         ).start()
 
     loop(1, n * m, send_row)
-    all_of(halves.at[others], half_s, half_r).wait_recv()
-    mine = pl.ds(tm * n, n)
-    fwd_copy = move(halves.at[mine], halves.at[mine], fwd_s, fwd_r, me, other)
-    fwd_copy.start()
     wide_copy.wait_recv()
     flip(wide_in, 1)
 
-    def narrow(i):
-        slabs[1, aligned(i, chunk), :] = wide_in[aligned(i, chunk), :].astype(BF16)
-
-    loop(0, 8, narrow)
     all_of(parts_in.at[others], part_s, part_r).wait_send()
-    all_of(halves.at[others], half_s, half_r).wait_send()
+    all_of(runs_all.at[others], half_s, half_r).wait_send()
     wide_copy.wait_send()
     all_of(times_all.at[pl.ds(1, n * m - 1)], row_s, row_r).wait_recv()
     for k in range(n * m):
@@ -276,12 +266,21 @@
         piece = flipped[aligned(to_z, strip), :]
         terms[pl.ds(to_z * QUAD, QUAD)] = fold(dot_low(piece, weight)).reshape(QUAD, block, rank)
         loop(max(k * QUAD, 1), (k + 1) * QUAD, send_term)
+    rest_copy.start()
     all_of(times_all.at[pl.ds(1, n * m - 1)], row_s, row_r).wait_send()
-    fwd_copy.wait()
-    run_gram = self_gram(halves[...].reshape(n * m * half, rank))
     time_gram = self_gram(times_flat[...])
     own = bin_ref[aligned(flat, block), :]
     scale = own / dot_f32(own, run_gram * time_gram)
+
+    def narrow(core):
+        def step(i):
+            slabs[1, aligned(i, chunk), aligned(core, span)] = wide_in[
+                core, aligned(i, chunk), :
+            ].astype(BF16)
+
+        loop(0, 8, step)
+
+    narrow(tm)
     gram_sum[...] = jnp.zeros_like(gram_sum)
     inner_sum[...] = jnp.zeros_like(inner_sum)
     total = terms[me]
@@ -296,6 +295,8 @@
         ).start()
 
     loop(1, n, send_bins)
+    rest_copy.wait()
+    narrow(other)
     all_of(terms_in.at[others], term_s, term_r).wait_send()
 
     def group(core, k):
@@ -340,7 +341,7 @@
     run_out[...] = runs * run_terms / (dot_f32(runs, gram_sum[...] * time_gram) + 1.0 - live)
     time_out[...] = times_flat[aligned(tm, kk), :]
     all_of(bins_all.at[others], bin_s, bin_r.at[0]).wait_send()
-    all_of(bins_all.at[mine], pass_s, pass_r.at[0]).wait_send()
+    all_of(bins_all.at[pl.ds(0, n)], pass_s, pass_r.at[0]).wait_send()
 
     def finish(k):
         for core in range(m):
@@ -371,7 +372,6 @@
     rows, kk, jj = tensor.shape
     rank = bin_init.shape[1]
     block = jj // (n * m)
-    half = rows // m
     zs = n // QUAD
     dma = pltpu.SemaphoreType.DMA
     vmem = pl.BlockSpec(memory_space=pltpu.VMEM)
@@ -392,20 +392,20 @@
             pltpu.VMEM((rows, rank), F32),
             pltpu.VMEM((jj, rank), F32),
             pltpu.VMEM((kk, rank), F32),
-            pltpu.VMEM((rows * kk, jj), F32),
-            pltpu.VMEM((rows * kk, jj), F32),
+            pltpu.VMEM((m, rows * kk, jj // m), F32),
+            pltpu.VMEM((m, rows * kk, jj // m), F32),
             pltpu.VMEM((jj // m, m * rows * kk), BF16),
             pltpu.VMEM((n, block, rank), F32),
             pltpu.VMEM((n, block, rank), F32),
             pltpu.VMEM((n * m, block, rank), F32),
             pltpu.VMEM((m, rows * kk, rank), F32),
             pltpu.VMEM((rank, rank), F32),
-            pltpu.VMEM((n * m, half, rank), F32),
-            pltpu.VMEM((n, 1, 2 * rank), F32),
-            pltpu.VMEM((n, 1, 2 * rank), F32),
+            pltpu.VMEM((n, rows, rank), F32),
+            pltpu.VMEM((n, 1, rank), F32),
+            pltpu.VMEM((n, 1, rank), F32),
             pltpu.VMEM((n * m, 1, rank), F32),
             pltpu.VMEM((n * m, rank), F32),
-            dma((5,)), *[dma] * 12, dma, dma((zs,)), dma, dma((zs,)), dma((zs, m)),
+            dma((5,)), dma((2,)), dma((2,)), *[dma] * 8, dma, dma((zs,)), dma, dma((zs,)), dma((zs, m)),
         ],
         compiler_params=pltpu.CompilerParams(
             collective_id=0, has_side_effects=True, vmem_limit_bytes=VMEM_LIMIT
@@ -424,7 +424,7 @@
 
 def update(n, m, *args):
     rows, kk, jj = args[0].shape
-    fits = m == 2 and kk == n and n % QUAD == 0 and kk % 16 == 0 and rows % (8 * m) == 0
+    fits = m == 2 and kk == n and n % QUAD == 0 and kk % 16 == 0 and rows % 8 == 0
     fits = fits and jj % (8 * n * m) == 0 and (QUAD * jj // (n * m)) % 128 == 0
     return fused(n, m, *args) if fits else shards(*args)
 

time: 36 us -> 37.5 us (1.042)
  Pallas kernels: 34.5 us -> 36 us
    pallas_call x1, Pallas kernels: 32.6 us -> 34.1 us  [fused(): pl.pallas_call(functools.partial(kernel, n, m), out_shape=shapes, in_spec...]
where the time goes in v7:
time: 37.5 us; the launch traced here: 37.3 us
  Pallas kernels  36 us (96%)
  between operations  1.28 us (3%)
    pallas_call x1, Pallas kernels, fused(): pl.pallas_call(functools.partial(kernel, n, m), out_shape=shapes, in_spec...  34.1 us
    pallas_call x1, Pallas kernels, fused(): pl.pallas_call(hand_out, out_shape=shapes, in_specs=[anywhere] * 3, out_s...  1.89 us

profile of v7, /device:TPU:1, one launch (start us, length us, event | category | flops | bytes accessed | tf_op | source)
XLA Modules:
  0.0 37.3 jit_solution(4799023636037321766)
XLA Ops:
  1.3 34.1 %shard_map.76 = (f32[16,128]{1,0:T(8,128)}, f32[32,32,128]{2,1,0:T(8,128)}, f32[16,128]{1,0:T(8,128)}) custom-call(s32[1]{0:T(128)S(6)} %copy.8.count_in, bf16[256,1024]{1,0:T(8,128)(2,1)} %bitcast.2, f32[16,128]{1,0:T(8,128)} %run_in.1, f32[1024,128]{1,0:T(8,128)} %bin_in.1, f32[16,128]{1,0:T(8,128)} %time_in.1), custom_call_target="tpu_custom_call" | custom-call | tf_op jit(solution)/shard_map/pallas_call | solution.py:384
  35.4 1.9 %shard_map.77 = (f32[16,128]{1,0:T(8,128)}, f32[32,32,128]{2,1,0:T(8,128)}, f32[16,128]{1,0:T(8,128)}) custom-call(f32[16,128]{1,0:T(8,128)} %get-tuple-element.9.run_in, f32[32,32,128]{2,1,0:T(8,128)} %get-tuple-element.10.bin_in, f32[16,128]{1,0:T(8,128)} %get-tuple-element.11.time_in), custom_call_target="tpu_custom_call" | custom-call | tf_op jit(solution)/shard_map/pallas_call | solution.py:414

commit v8 on v4

--- a/solution.py
+++ b/solution.py
@@ -184,13 +184,7 @@
     upper = inner[0] * runs[0:1]
     for i in range(1, rows):
         upper = upper + inner[i] * runs[i:i + 1]
-    gram_sum[...] = jnp.zeros_like(gram_sum)
-
-    def gram_step(i):
-        gram_sum[...] += self_gram(bin_ref[aligned(i, jj // zs), :])
-
-    loop(0, zs, gram_step)
-    lower = dot_f32(time_ref[...], self_gram(runs) * gram_sum[...])
+    lower = dot_f32(time_ref[...], self_gram(runs) * self_gram(bin_ref[...]))
     both = jnp.concatenate([upper, lower], axis=1)
     for k in range(kk):
         parts[k] = both[k:k + 1]
@@ -250,10 +244,6 @@
     wide_copy.wait_recv()
     flip(wide_in, 1)
 
-    def narrow(i):
-        slabs[1, aligned(i, chunk), :] = wide_in[aligned(i, chunk), :].astype(BF16)
-
-    loop(0, 8, narrow)
     all_of(parts_in.at[others], part_s, part_r).wait_send()
     all_of(halves.at[others], half_s, half_r).wait_send()
     wide_copy.wait_send()
@@ -282,6 +272,11 @@
     time_gram = self_gram(times_flat[...])
     own = bin_ref[aligned(flat, block), :]
     scale = own / dot_f32(own, run_gram * time_gram)
+
+    def narrow(i):
+        slabs[1, aligned(i, chunk), :] = wide_in[aligned(i, chunk), :].astype(BF16)
+
+    loop(0, 8, narrow)
     gram_sum[...] = jnp.zeros_like(gram_sum)
     inner_sum[...] = jnp.zeros_like(inner_sum)
     total = terms[me]

time: 36 us -> 35.9 us (level)
  no operation moved by 1% of the time
where the time goes in v8:
time: 35.9 us; the launch traced here: 35.6 us
  Pallas kernels  34.4 us (96%)
  between operations  1.28 us (4%)
    pallas_call x1, Pallas kernels, fused(): pl.pallas_call(functools.partial(kernel, n, m), out_shape=shapes, in_spec...  32.5 us
    pallas_call x1, Pallas kernels, fused(): pl.pallas_call(hand_out, out_shape=shapes, in_specs=[anywhere] * 3, out_s...  1.89 us

profile of v8, /device:TPU:1, one launch (start us, length us, event | category | flops | bytes accessed | tf_op | source)
XLA Modules:
  0.0 35.6 jit_solution(14796166028846431279)
XLA Ops:
  1.3 32.5 %shard_map.76 = (f32[16,128]{1,0:T(8,128)}, f32[32,32,128]{2,1,0:T(8,128)}, f32[16,128]{1,0:T(8,128)}) custom-call(s32[1]{0:T(128)S(6)} %copy.8.count_in, bf16[256,1024]{1,0:T(8,128)(2,1)} %bitcast.2, f32[16,128]{1,0:T(8,128)} %run_in.1, f32[1024,128]{1,0:T(8,128)} %bin_in.1, f32[16,128]{1,0:T(8,128)} %time_in.1), custom_call_target="tpu_custom_call" | custom-call | tf_op jit(solution)/shard_map/pallas_call | solution.py:379
  33.7 1.9 %shard_map.77 = (f32[16,128]{1,0:T(8,128)}, f32[32,32,128]{2,1,0:T(8,128)}, f32[16,128]{1,0:T(8,128)}) custom-call(f32[16,128]{1,0:T(8,128)} %get-tuple-element.9.run_in, f32[32,32,128]{2,1,0:T(8,128)} %get-tuple-element.10.bin_in, f32[16,128]{1,0:T(8,128)} %get-tuple-element.11.time_in), custom_call_target="tpu_custom_call" | custom-call | tf_op jit(solution)/shard_map/pallas_call | solution.py:409

commit v9 on v8

--- a/solution.py
+++ b/solution.py
@@ -149,8 +149,8 @@
     def all_of(ref, send, recv):
         return move(ref, ref, send, recv, me, other)
 
-    def loop(low, high, body):
-        lax.fori_loop(low, high, lambda i, c: (body(i), c)[1], 0)
+    def loop(low, high, body, unroll=1):
+        lax.fori_loop(low, high, lambda i, c: (body(i), c)[1], 0, unroll=unroll)
 
     def aligned(value, unit):
         return pl.ds(pl.multiple_of(value * unit, unit), unit)
@@ -195,7 +195,7 @@
         peer = lax.rem(me + off, n)
         move(parts.at[peer], parts_in.at[off], part_s, part_r, peer, tm).start()
 
-    loop(1, n, send_part)
+    loop(1, n, send_part, 5 if n % 5 == 1 else 1)
 
     chunk = rows * kk // 8
 
@@ -265,7 +265,7 @@
         to_z = lax.rem(z + k, zs)
         piece = flipped[aligned(to_z, strip), :]
         terms[pl.ds(to_z * QUAD, QUAD)] = fold(dot_low(piece, weight)).reshape(QUAD, block, rank)
-        loop(max(k * QUAD, 1), (k + 1) * QUAD, send_term)
+        loop(max(k * QUAD, 1), (k + 1) * QUAD, send_term, QUAD if k else QUAD - 1)
     all_of(times_all.at[pl.ds(1, n * m - 1)], row_s, row_r).wait_send()
     fwd_copy.wait()
     run_gram = self_gram(halves[...].reshape(n * m * half, rank))
@@ -290,7 +290,7 @@
             bins_all.at[flat], bins_all.at[flat], bin_s, bin_r.at[index // QUAD], ahead(index), tm
         ).start()
 
-    loop(1, n, send_bins)
+    loop(1, n, send_bins, 5 if n % 5 == 1 else 1)
     all_of(terms_in.at[others], term_s, term_r).wait_send()
 
     def group(core, k):

time: 35.9 us -> 35.8 us (level)
  no operation moved by 1% of the time
where the time goes in v9:
time: 35.8 us; the launch traced here: 35.6 us
  Pallas kernels  34.3 us (96%)
  between operations  1.28 us (4%)
    pallas_call x1, Pallas kernels, fused(): pl.pallas_call(functools.partial(kernel, n, m), out_shape=shapes, in_spec...  32.5 us
    pallas_call x1, Pallas kernels, fused(): pl.pallas_call(hand_out, out_shape=shapes, in_specs=[anywhere] * 3, out_s...  1.89 us

profile of v9, /device:TPU:1, one launch (start us, length us, event | category | flops | bytes accessed | tf_op | source)
XLA Modules:
  0.0 35.6 jit_solution(9167137927233978350)
XLA Ops:
  1.3 32.5 %shard_map.76 = (f32[16,128]{1,0:T(8,128)}, f32[32,32,128]{2,1,0:T(8,128)}, f32[16,128]{1,0:T(8,128)}) custom-call(s32[1]{0:T(128)S(6)} %copy.8.count_in, bf16[256,1024]{1,0:T(8,128)(2,1)} %bitcast.2, f32[16,128]{1,0:T(8,128)} %run_in.1, f32[1024,128]{1,0:T(8,128)} %bin_in.1, f32[16,128]{1,0:T(8,128)} %time_in.1), custom_call_target="tpu_custom_call" | custom-call | tf_op jit(solution)/shard_map/pallas_call | solution.py:379
  33.7 1.9 %shard_map.77 = (f32[16,128]{1,0:T(8,128)}, f32[32,32,128]{2,1,0:T(8,128)}, f32[16,128]{1,0:T(8,128)}) custom-call(f32[16,128]{1,0:T(8,128)} %get-tuple-element.9.run_in, f32[32,32,128]{2,1,0:T(8,128)} %get-tuple-element.10.bin_in, f32[16,128]{1,0:T(8,128)} %get-tuple-element.11.time_in), custom_call_target="tpu_custom_call" | custom-call | tf_op jit(solution)/shard_map/pallas_call | solution.py:409
